TPU v7x, 32 devices: a whole 2x2x4 slice. The times are simulated.
32 devices in a mesh: section: 2 (over core), dp: 16 (over z, y, x).
Axes of the slice: x: 2, y: 2, z: 4, core: 2. Of those that a mesh axis runs over, the one named last changes fastest.
Arguments:
- features: float32 [2, 19200, 512], P('section', 'dp'), may hold values from -6 to 6
- out_grad: float32 [2, 19200, 512], P('section', 'dp'), may hold values from -6 to 6
- lengths: int32 [2, 16, 3], P('section', 'dp'), may hold values from 100 to 400, as said below
- join_pick: int32 [16, 3], P('dp'), may hold values from 0 to 2, each once within a row
- dw_weight: float32 [2, 5, 5, 512], P('section'), may hold values from -2.5 to 2.5
- pw_weight: float32 [2, 5, 512, 512], P('section'), may hold values from -0.25 to 0.25
- bn_gain: float32 [2, 6, 512], P('section'), may hold values from 0.5 to 1.5
- bn_bias: float32 [2, 6, 512], P('section'), may hold values from -2 to 2
- res_weight: float32 [2, 512, 512], P('section'), may hold values from -0.25 to 0.25
- se_down: float32 [2, 512, 64], P('section'), may hold values from -0.5 to 0.5
- se_down_bias: float32 [2, 64], P('section'), may hold values from -2.5 to 2.5
- se_up: float32 [2, 64, 512], P('section'), may hold values from -1.5 to 1.5
- se_up_bias: float32 [2, 512], P('section'), may hold values from -2.5 to 2.5
Outputs:
- block_out: float32 [2, 19200, 512], P('section', 'dp')
- features_grad: float32 [2, 19200, 512], P('section', 'dp')
- dw_weight_grad: float32 [2, 5, 5, 512], P('section')
- pw_weight_grad: float32 [2, 5, 512, 512], P('section')
- bn_gain_grad: float32 [2, 6, 512], P('section')
- bn_bias_grad: float32 [2, 6, 512], P('section')
- res_weight_grad: float32 [2, 512, 512], P('section')
- se_down_grad: float32 [2, 512, 64], P('section')
- se_down_bias_grad: float32 [2, 64], P('section')
- se_up_grad: float32 [2, 64, 512], P('section')
- se_up_bias_grad: float32 [2, 512], P('section')
Inputs may be any that keep to these rules, and one draw needn't show every extreme that they name: `lengths`: row 0 lies between 200 and 400, row 1 between 100 and 200; each of these four ends is taken by some entry. `join_pick`: each row is a permutation of the 3 slots.
All inputs are finite; a program needn't handle non-finite values.
Results may differ from a plain program's by a relative error of at most 0.0003.
Values sent between devices are 32-bit elements; how exact they have to be, the bound alone decides.
No kernel may reach another device: no remote copies, remote signals or barrier semaphores. Data moves between devices by JAX's collectives and lax.ppermute only.
A program may use at most 320 MiB of HBM per device.

v0:
```python
import copy

import jax
import jax.numpy as jnp
from jax import lax
from jax.experimental import pallas as pl
from jax.experimental.pallas import tpu as pltpu
from jax.sharding import PartitionSpec as P

EPSILON = 1e-05
EXACT = lax.Precision.HIGHEST
TAPS = 5
MB = 3
OWN = 2
SLOT = 400
HALF = 200
KEPT = 208
C = 512
LANES = 128
CHUNKS = [slice(c, c + LANES) for c in range(0, C, LANES)]
SE = 64
BF16, F32 = jnp.bfloat16, jnp.float32
VMEM_BYTES = 60 << 20
TAIL_ROWS = 2 * SE + 8
SMALL = 256


def radices(size, most):
    stages, left = [], size
    while left > 1:
        radix = min(most, left)
        while left % radix:
            radix -= 1
        stages.append(radix)
        left //= radix
    return stages


def exchange(block, radix, stride):
    size = lax.axis_size("dp")
    if radix == size:
        return lax.all_to_all(block, "dp", 0, 0)
    groups = []
    for base in range(size):
        if (base // stride) % radix == 0:
            groups.append([base + j * stride for j in range(radix)])
    return lax.all_to_all(block, "dp", 0, 0, axis_index_groups=groups)


def shared(block, stages):
    stride = 1
    for no, radix in enumerate(stages):
        if no:
            block = jnp.broadcast_to(jnp.sum(block, axis=0), (radix,) + block.shape[1:])
        block = exchange(block, radix, stride)
        stride *= radix
    return block


def halves(x):
    high = x.astype(BF16)
    return high, (x - high.astype(F32)).astype(BF16)


def sigmoid(x):
    return 0.5 * jnp.tanh(0.5 * x) + 0.5


def exact_dot(a, b, dims=((1,), (0,))):
    return lax.dot_general(a, b, (dims, ((), ())), precision=EXACT, preferred_element_type=F32)


def fast_dot(a, b, dims=((1,), (0,))):
    return lax.dot_general(a, b, (dims, ((), ())), preferred_element_type=F32)


def stacked_dot(high, low, w, back=False):
    w_high, w_low = w[0], w[1]
    w = jnp.concatenate([w_high, w_high, w_low], axis=1 if back else 0)
    x = jnp.concatenate([high, low, high], axis=1)
    return fast_dot(x, w, ((1,), (1 if back else 0,)))


def stacked_outer(a_high, a_low, b_high, b_low):
    a = jnp.concatenate([a_high, a_low, a_high], axis=0)
    b = jnp.concatenate([b_high, b_high, b_low], axis=0)
    return fast_dot(a, b, ((0,), (0,)))


def column_sum(x):
    return jnp.sum(x, axis=0, keepdims=True)


class Rows:
    def __init__(self, meta, m, two, rows, which=0):
        place = lax.broadcasted_iota(jnp.int32, (rows, LANES), 0)
        if two:
            later = place >= HALF
            limit = jnp.where(later, HALF + meta[OWN + m], meta[m])
            self.mask = place < limit
        else:
            self.mask = place < meta[which * OWN + m]

    def keep(self, x):
        return jnp.where(self.mask, x, 0.0)


class Padded:
    def __init__(self, ref, two):
        self.ref = ref
        self.pieces = [(8, 0, HALF), (16 + HALF, HALF, HALF)] if two else [(8, 0, SLOT)]

    def put(self, x):
        zeros = jnp.zeros((8, LANES), F32)
        for at, start, rows in self.pieces:
            self.ref[at - 8 : at, :] = zeros
            self.ref[at : at + rows, :] = x[start : start + rows]
        self.ref[at + rows : at + rows + 8, :] = zeros

    def get(self, offset):
        parts = [self.ref[at + offset : at + offset + rows, :] for at, _, rows in self.pieces]
        return parts[0] if len(parts) == 1 else jnp.concatenate(parts, axis=0)

    def conv(self, kernel):
        total = kernel[0:1] * self.get(-2)
        for k in range(1, TAPS):
            total = total + kernel[k : k + 1] * self.get(k - 2)
        return total

    def conv_back(self, kernel):
        total = kernel[0:1] * self.get(2)
        for k in range(1, TAPS):
            total = total + kernel[k : k + 1] * self.get(2 - k)
        return total


def every_other(ref, x):
    ref[0:SLOT, :] = x
    ref[SLOT : 2 * KEPT, :] = jnp.zeros((2 * KEPT - SLOT, LANES), F32)
    return ref[pl.ds(0, KEPT, stride=2), :]


def spread_out(ref, x):
    ref[...] = jnp.zeros_like(ref)
    ref[pl.ds(0, KEPT, stride=2), :] = x
    return ref[0:SLOT, :]


def center_spread(sums, rows):
    center = sums[0:1] / rows
    return center, lax.rsqrt(sums[1:2] / rows - center * center + EPSILON)


def added(ref):
    return jnp.sum(ref[:, 0], axis=0)


def accumulate(ref, m, at, value):
    rows = slice(at, at + value.shape[0])
    ref[rows, :] = jnp.where(m == 0, value, ref[rows, :] + value)


def send(ref, rows):
    for copy in range(ref.shape[0]):
        for row, x in enumerate(rows):
            ref[copy, 0, row : row + 1, 0 : x.shape[1]] = x


def pad_scratch():
    return pltpu.VMEM((len(CHUNKS), SLOT + 24, LANES), F32)


def stride_scratch():
    return pltpu.VMEM((len(CHUNKS), 2 * KEPT, LANES), F32)


def slots(rows, cols=C):
    return pl.BlockSpec((1, rows, cols), lambda m, *_: (m, 0, 0))


def copies(count, rows, cols=C):
    return pl.BlockSpec((count, 1, rows, cols), lambda m, *_: (0, m, 0, 0))


def whole(*shape):
    return pl.BlockSpec(shape, lambda m, *_: (0,) * len(shape))


def layer(i, *shape):
    return pl.BlockSpec((1,) + shape, lambda m, *_: (i,) + (0,) * len(shape))


def f32(*shape):
    return jax.ShapeDtypeStruct(shape, F32)


def bf16(*shape):
    return jax.ShapeDtypeStruct(shape, BF16)


def call(body, meta, args, outs, scratch=(), name=None, flops=0, steps=OWN, after=(), into=()):
    arrays, in_specs = [a for a, _ in args], [s for _, s in args]
    shapes, out_specs = [a for a, _ in outs], [s for _, s in outs]
    size = sum(a.size * a.dtype.itemsize for a in arrays + shapes)
    extra = list(after) + list(into)
    count = len(arrays)

    def inner(meta, *refs):
        body(meta, *refs[:count], *refs[count + len(extra) :])

    return pl.pallas_call(
        inner,
        out_shape=shapes,
        grid_spec=pltpu.PrefetchScalarGridSpec(
            num_scalar_prefetch=1,
            grid=(steps,),
            in_specs=in_specs + [pl.BlockSpec(memory_space=pl.ANY)] * len(extra),
            out_specs=out_specs,
            scratch_shapes=list(scratch),
        ),
        input_output_aliases={1 + count + len(after) + j: j for j in range(len(into))},
        compiler_params=pltpu.CompilerParams(vmem_limit_bytes=VMEM_BYTES),
        cost_estimate=pl.CostEstimate(flops=flops, bytes_accessed=size, transcendentals=0),
        name=name,
    )(meta, *arrays, *extra)


class Linked:
    def __init__(self, index, rows):
        self.index, self.rows = index, rows


class Part:
    def __init__(self, ref, at):
        self.ref, self.at = ref, at

    def __getitem__(self, index):
        return self.ref[self.at + index]


def run(steps):
    body, meta, args, outs, scratch, name, flops, after, into = next(steps)
    return finish(steps, call(body, meta, args, outs, scratch, name, flops, after=after, into=into))


def finish(steps, results):
    try:
        steps.send(results)
    except StopIteration as stop:
        return stop.value


def run_joined(one, two, scalars):
    meta, at1, at2 = scalars
    body1, _, args1, outs1, scratch1, name1, flops1, after1, into1 = next(one)
    body2, _, args2, outs2, scratch2, name2, flops2, after2, into2 = next(two)
    assert not into2
    own2 = [arg for arg in args2 if not isinstance(arg[0], Linked)]
    sizes = len(args1), len(own2), len(outs1), len(outs2), len(scratch1), len(scratch2)

    def body(meta, *refs):
        refs = list(refs)
        in1, in2, out1, out2, scr1, scr2 = [[refs.pop(0) for _ in range(n)] for n in sizes]
        body1(Part(meta, at1), *in1, *out1, *scr1)
        linked = []
        for arg in args2:
            link = arg[0]
            linked.append(out1[link.index].at[:, 0 : link.rows, :] if isinstance(link, Linked) else in2.pop(0))
        body2(Part(meta, at2), *linked, *out2, *scr2)

    def moved(spec, at):
        if spec.index_map is None:
            return spec
        return pl.BlockSpec(spec.block_shape, lambda m, meta: spec.index_map(m, Part(meta, at)))

    args = [(a, moved(spec, at1)) for a, spec in args1] + [(a, moved(spec, at2)) for a, spec in own2]
    results = call(
        body, meta, args, [(a, moved(spec, at1)) for a, spec in outs1] + [(a, moved(spec, at2)) for a, spec in outs2], list(scratch1) + list(scratch2), f"{name1}_{name2}", flops1 + flops2,
        after=(*after1, *after2), into=into1,
    )
    return finish(one, results[: len(outs1)]), finish(two, results[len(outs1) :])


def choose(meta, block, own, far):
    return jnp.where(meta[2 * OWN] == 1 - block, own, far)


def prepare(meta, own, far, block, start, stop):
    def body(meta, *refs):
        pair = [ref[0] for ref in refs[:2]]
        if stop == 6:
            last = pl.program_id(0) == 5 - start
            pair = [jnp.where(last, ref[...], w) for ref, w in zip(refs[2:4], pair)]
        out = refs[-1]
        out[0, 0], out[0, 1] = halves(choose(meta, block, *pair))

    matrix = pl.BlockSpec((1, C, C), lambda j, *_: (jnp.minimum(j + start, 4), 0, 0))
    args = [(own[0], matrix), (far[0], matrix)]
    if stop == 6:
        args += [(own[1], whole(C, C)), (far[1], whole(C, C))]
    out = pl.BlockSpec((1, 2, C, C), lambda j, *_: (j, 0, 0, 0))
    name = f"prepare_{block}_{start}"
    return call(body, meta, args, [(bf16(stop - start, 2, C, C), out)], name=name, steps=stop - start)[0]


class Block:
    def __init__(self, two, meta, weights, ready, stages):
        self.done, self.stop, self.pending = (), None, None
        self.two, self.meta, self.stages = two, meta, stages
        self.dw, self.gain, self.bias = weights
        self.ready = ready
        self.tail_rows = SLOT if two else KEPT
        self.first, self.last = stages[0], stages[-1]
        self.tag = "c15" if two else "c14"

    def rows_of(self, i):
        return self.tail_rows if i == 4 else SLOT

    def valid(self, meta, m, i):
        last = i == 4 and not self.two
        return Rows(meta, m, self.two, self.rows_of(i), which=1 if last else 0)

    def matrix(self, i):
        array, at = self.ready[i]
        return (array, layer(at, 2, C, C))

    def source_args(self):
        if not self.two:
            return [(self.x, slots(SLOT)), (self.x_far, whole(SLOT, C))]
        far = pl.BlockSpec((HALF, C), lambda m, *_: (m, 0))
        near = pl.BlockSpec((1, 1, HALF, C), lambda m, meta: (meta[2 * OWN + 1], 1, 0, 0))
        return [(self.arrived, slots(HALF)), (self.joined_far, far), (self.joined, near)]

    def source(self, meta, refs, cs):
        lower = meta[2 * OWN] == 1
        if not self.two:
            return jnp.where(lower, refs[0][0, :, cs], refs[1][:, cs])
        joined = jnp.where(lower, refs[1][:, cs], refs[2][0, 0, :, cs])
        return jnp.concatenate([refs[0][0, :, cs], joined], axis=0)

    def before_args(self, i):
        if i == 0:
            return self.source_args()
        return [(self.z[i - 1], slots(SLOT)), (self.stats[i - 1], slots(2))]


    def forward_layer(self, i, after=()):
        return run(self.forward_steps(i, after))

    def forward_steps(self, i, after=()):
        two, count = self.two, self.first
        strided = i == 4 and not two
        rows = self.rows_of(i)
        n_src = len(self.source_args())
        width = C + LANES if i == 0 else C
        sent = 4 if i == 3 else 2
        makes = i == 0 and not two

        def body(meta, *refs):
            refs = list(refs)
            take = lambda n: [refs.pop(0) for _ in range(n)]
            m = pl.program_id(0)
            if i == 0:
                src = take(n_src)
            else:
                z_ref, got_ref = take(2)
                n_ref, = take(1) if i > 1 else (None,)
                gain_ref, bias_ref = take(2)
                res_sum, = take(1) if i == 3 else (None,)
            dw_ref, = take(1)
            if makes:
                own_ref, far_ref, z_out, pay, w_ref = take(5)

                @pl.when(m == 0)
                def _():
                    w_ref[0, 0], w_ref[0, 1] = halves(choose(meta, 0, own_ref[0], far_ref[0]))

            else:
                w_ref, z_out, pay = take(3)
            if i:
                stat_out, = take(1)
            if i == 1:
                n_out, = take(1)
            pad, y_ref = take(2)
            alt, = take(1) if strided else (None,)
            valid_in = self.valid(meta, m, 0)
            if i:
                sums = added(got_ref)
                if i == 1:
                    count_in = jnp.maximum(jnp.concatenate([sums[0:1, C:]] * len(CHUNKS), axis=1), 1.0)
                    count_out = jnp.maximum(jnp.concatenate([sums[1:2, C:]] * len(CHUNKS), axis=1), 1.0)
                    n_out[0, 0:1, :] = count_in
                    n_out[0, 1:2, :] = count_out
                else:
                    count_in = n_ref[0, 0:1, :]
                center, spread = center_spread(sums[:, :C], count_in)
                stat_out[0, 0:1, :] = center
                stat_out[0, 1:2, :] = spread
                scale = gain_ref[i - 1 : i] * spread
                shift = bias_ref[i - 1 : i] - center * scale
            for c, cs in enumerate(CHUNKS):
                if i == 0:
                    h = valid_in.keep(self.source(meta, src, cs))
                else:
                    u = z_ref[0, :, cs] * scale[:, cs] + shift[:, cs]
                    h = valid_in.keep(u * sigmoid(u))
                padded = Padded(pad.at[c], two)
                padded.put(h)
                y = padded.conv(dw_ref[0, :, cs])
                if strided:
                    y = every_other(alt.at[c], y)
                high, low = halves(y)
                y_ref[:, cs] = high
                y_ref[:, C + cs.start : C + cs.stop] = low
            w = w_ref.at[0] if makes else w_ref.at[0]
            z = stacked_dot(y_ref[:, 0:C], y_ref[:, C : 2 * C], w)
            z_out[0] = z
            valid = self.valid(meta, m, i)
            one, square = [], []
            for cs in CHUNKS:
                kept = valid.keep(z[:, cs])
                one.append(column_sum(kept))
                square.append(column_sum(kept * kept))
            if i == 0:
                if two:
                    number = (meta[m] + meta[OWN + m]).astype(F32)
                    numbers = number, number
                else:
                    numbers = meta[m].astype(F32), meta[OWN + m].astype(F32)
                one.append(jnp.full((1, LANES), numbers[0], F32))
                square.append(jnp.full((1, LANES), numbers[1], F32))
            out = [jnp.concatenate(one, axis=1), jnp.concatenate(square, axis=1)]
            if i == 3:
                out += [res_sum[0, 0:1, :], res_sum[0, 1:2, :]]
            send(pay, out)

        if i == 0:
            args = list(self.source_args())
        else:
            got = 4 if i == 4 else 2
            args = [(self.z[i - 1], slots(SLOT)), (self.got[i - 1], copies(self.last, got, C + LANES if i == 1 else C))]
            if i > 1:
                args.append((self.number, slots(2)))
            args += [(self.gain, whole(6, C)), (self.bias, whole(6, C))]
            if i == 3:
                args.append((self.res_sum, slots(2)))
        args.append((self.dw, layer(i, TAPS, C)))
        args += [(w, layer(0, C, C)) for w in self.first_matrix] if makes else [self.matrix(i)]
        outs = [(f32(OWN, rows, C), slots(rows)), (f32(count, OWN, sent, width), copies(count, sent, width))]
        if i:
            outs.append((f32(OWN, 2, C), slots(2)))
        if i == 1:
            outs.append((f32(OWN, 2, C), slots(2)))
        if makes:
            outs.append((bf16(1, 2, C, C), layer(0, 2, C, C)))
        scratch = [pad_scratch(), pltpu.VMEM((rows, 2 * C), BF16)]
        if strided:
            scratch.append(stride_scratch())
        flops = 6 * OWN * rows * C * C
        result = yield body, self.meta, args, outs, scratch, f"{self.tag}_forward_{i}", flops, after, ()
        self.z.append(result[0])
        if makes:
            self.ready[0] = (result[2], 0)
        if i:
            self.stats.append(result[2])
        if i == 1:
            self.number = result[3]
        self.got.append(shared(result[1], self.stages))

    def residual(self):
        two, rows = self.two, self.tail_rows

        def body(meta, *refs):
            refs = list(refs)
            src = [refs.pop(0) for _ in self.source_args()]
            w_ref, r_out, x_out, sum_out = refs[:4]
            alt = refs[4] if not two else None
            m = pl.program_id(0)
            valid_in = self.valid(meta, m, 0)
            for c, cs in enumerate(CHUNKS):
                x = valid_in.keep(self.source(meta, src, cs))
                if not two:
                    x = every_other(alt.at[c], x)
                high, low = halves(x)
                x_out[0, :, cs] = high
                x_out[0, :, C + cs.start : C + cs.stop] = low
            r = stacked_dot(x_out[0, :, 0:C], x_out[0, :, C : 2 * C], w_ref.at[0])
            r_out[0] = r
            valid = self.valid(meta, m, 4)
            for cs in CHUNKS:
                kept = valid.keep(r[:, cs])
                sum_out[0, 0:1, cs] = column_sum(kept)
                sum_out[0, 1:2, cs] = column_sum(kept * kept)

        args = self.source_args() + [self.matrix(5)]
        outs = [
            (f32(OWN, rows, C), slots(rows)),
            (bf16(OWN, rows, 2 * C), slots(rows, 2 * C)),
            (f32(OWN, 2, C), slots(2)),
        ]
        scratch = [] if two else [stride_scratch()]
        self.r, self.picked, self.res_sum = call(
            body, self.meta, args, outs, scratch, f"{self.tag}_residual", 6 * OWN * rows * C * C
        )

    def start(self):
        self.z, self.got, self.stats = [], [], []

    def forward(self, after=None, joined=False):
        if not joined:
            self.start()
        for i in range(1 if joined else 0, 5):
            if i == 2:
                self.residual()
            self.forward_layer(i, (after or {}).get(i, ()))


    def segments(self):
        return [(0, HALF), (HALF, HALF)] if self.two else [(0, self.tail_rows)]

    def lengths(self, meta, m):
        if self.two:
            return [meta[m], meta[OWN + m]]
        return [meta[OWN + m]]

    def squeeze(self, sums, counts, se_refs):
        down_t, down_b, up, up_b = se_refs
        means = [s / jnp.maximum(jnp.full((1, C), n.astype(F32)), 1.0) for s, n in zip(sums, counts)]
        ps = [jnp.sum(down_t[...] * mean, axis=1, keepdims=True) + down_b[...] for mean in means]
        gates = [sigmoid(column_sum(up[...] * (p * sigmoid(p))) + up_b[...]) for p in ps]
        return means, ps, gates

    def squeeze_back(self, des, ps, gates, counts, se_refs, means, small, m):
        down_t, down_b, up, up_b = se_refs
        shares, up_grad, down_grad, dq_sum, dp_sum = [], 0.0, 0.0, 0.0, 0.0
        for de, p, gate, n, mean in zip(des, ps, gates, counts, means):
            dq = de * gate * (1.0 - gate)
            s = sigmoid(p)
            dp = jnp.sum(up[...] * dq, axis=1, keepdims=True) * (s * (1.0 + p * (1.0 - s)))
            shares.append(column_sum(down_t[...] * dp) / jnp.maximum(jnp.full((1, C), n.astype(F32)), 1.0))
            up_grad, down_grad = up_grad + (p * s) * dq, down_grad + dp * mean
            dq_sum, dp_sum = dq_sum + dq, dp_sum + dp
        row, col = (lax.broadcasted_iota(jnp.int32, (SE, C), axis) for axis in (0, 1))
        dp_row = column_sum(jnp.where(row == col, dp_sum, 0.0))
        accumulate(small, m, 0, up_grad)
        accumulate(small, m, SE, down_grad)
        accumulate(small, m, 2 * SE, dq_sum)
        accumulate(small, m, 2 * SE + 1, dp_row)
        return shares

    def last_norm(self, m, dt_out, du_out, z_ref, slope_ref, gates, shares, center, spread, res_bias, res_gain, pay, small):
        bias_sum, gain_sum = [], []
        for cs in CHUNKS:
            dh = dt_out[0, :, cs] * self.by_segment(gates, cs) + self.by_segment(shares, cs)
            du = dh * slope_ref[:, cs]
            du_out[0, :, cs] = du
            bias_sum.append(column_sum(du))
            gain_sum.append(column_sum(du * ((z_ref[0, :, cs] - center[:, cs]) * spread[:, cs])))
        rows = [jnp.concatenate(x, axis=1) for x in (bias_sum, gain_sum, res_bias, res_gain)]
        send(pay, rows)
        for j, row in enumerate(rows):
            accumulate(small, m, 2 * SE + 2 + j, row)

    def se_args(self):
        return list(zip(self.excitation, (whole(SE, C), whole(SE, 1), whole(SE, C), whole(1, C))))

    def store_rows(self, ref, rows):
        ref[0] = jnp.concatenate(rows + [jnp.zeros((8 - len(rows), C), F32)], axis=0)

    def store_columns(self, ref, columns):
        ref[0] = jnp.zeros((SE, 8), F32)
        for j, column in enumerate(columns):
            ref[0, :, j : j + 1] = column

    def by_segment(self, rows, cs):
        parts = [jnp.broadcast_to(row[:, cs], (n, LANES)) for row, (_, n) in zip(rows, self.segments())]
        return parts[0] if len(parts) == 1 else jnp.concatenate(parts, axis=0)

    def seg_sums(self, x):
        return [column_sum(x[at : at + n]) for at, n in self.segments()]

    def tail(self, cotangent=None, far=None, after=()):
        return run(self.tail_steps(cotangent, far, after))

    def tail_steps(self, cotangent=None, far=None, after=()):
        two, rows = self.two, self.tail_rows
        back = cotangent is not None

        def body(meta, *refs):
            refs = list(refs)
            take = lambda n: [refs.pop(0) for _ in range(n)]
            m = pl.program_id(0)
            z_ref, got4, r_ref, got3, n_ref, gain, bias = take(7)
            se_refs = take(4)
            if back:
                cot_ref, far_ref = take(2)
            out, stat_out, rstat_out, means_out, p_out, gate_out = take(6)
            if back:
                small, du_out, dt_out, pay = take(4)
            h_ref, = take(1)
            if back:
                slope_ref, = take(1)
            valid = self.valid(meta, m, 4)
            number = n_ref[0, 1:2, :]
            center, spread = center_spread(added(got4), number)
            rcenter, rspread = center_spread(added(got3)[2:4], number)
            stat_out[0, 0:1, :] = center
            stat_out[0, 1:2, :] = spread
            rstat_out[0, 0:1, :] = rcenter
            rstat_out[0, 1:2, :] = rspread
            scale = gain[4:5] * spread
            shift = bias[4:5] - center * scale
            sums = []
            for cs in CHUNKS:
                u = z_ref[0, :, cs] * scale[:, cs] + shift[:, cs]
                s = sigmoid(u)
                h = valid.keep(u * s)
                h_ref[:, cs] = h
                if back:
                    slope_ref[:, cs] = valid.keep(s * (1.0 + u * (1.0 - s)))
                sums.append(self.seg_sums(h))
            sums = [jnp.concatenate([s[j] for s in sums], axis=1) for j in range(len(self.segments()))]
            counts = self.lengths(meta, m)
            means, ps, gates = self.squeeze(sums, counts, se_refs)
            self.store_rows(means_out, means)
            self.store_columns(p_out, ps)
            self.store_rows(gate_out, gates)
            res_gain, res_bias, gate_grad = [], [], []
            for cs in CHUNKS:
                h = h_ref[:, cs]
                rh = (r_ref[0, :, cs] - rcenter[:, cs]) * rspread[:, cs]
                t = h * self.by_segment(gates, cs) + gain[5:6, cs] * rh + bias[5:6, cs]
                s = sigmoid(t)
                out[0, 0:rows, cs] = valid.keep(t * s)
                if rows < SLOT:
                    out[0, rows:SLOT, cs] = jnp.zeros((SLOT - rows, LANES), F32)
                if back:
                    cot = jnp.where(meta[2 * OWN] == 1, far_ref[0, :, cs], cot_ref[0, :, cs])
                    dt = valid.keep(cot * (s * (1.0 + t * (1.0 - s))))
                    dt_out[0, :, cs] = dt
                    res_bias.append(column_sum(dt))
                    res_gain.append(column_sum(dt * rh))
                    gate_grad.append(self.seg_sums(dt * h))
            if not back:
                return
            des = [jnp.concatenate([g[j] for g in gate_grad], axis=1) for j in range(len(counts))]
            shares = self.squeeze_back(des, ps, gates, counts, se_refs, means, small, m)
            self.last_norm(m, dt_out, du_out, z_ref, slope_ref, gates, shares, center, spread, res_bias, res_gain, pay, small)

        args = [
            (self.z[4], slots(rows)), (self.got[4], copies(self.last, 2)), (self.r, slots(rows)),
            (self.got[3], copies(self.last, 4)), (self.number, slots(2)),
            (self.gain, whole(6, C)), (self.bias, whole(6, C)),
        ] + self.se_args()
        outs = [
            (f32(OWN, SLOT, C), slots(SLOT)), (f32(OWN, 2, C), slots(2)), (f32(OWN, 2, C), slots(2)),
            (f32(OWN, 8, C), slots(8)), (f32(OWN, SE, 8), slots(SE, 8)), (f32(OWN, 8, C), slots(8)),
        ]
        scratch = [pltpu.VMEM((rows, C), F32)]
        if back:
            args += [(cotangent, layer(MB - 1, SLOT, C)), (far, slots(SLOT))]
            outs += self.tail_outs()
            scratch.append(pltpu.VMEM((rows, C), F32))
        result = yield body, self.meta, args, outs, scratch, f"{self.tag}_tail", 0, after, ()
        self.stats.append(result[1])
        self.rstat, self.se_state = result[2], result[3:6]
        if back:
            self.tail_results(result[6:])
        return result[0]

    def tail_outs(self):
        rows, count = self.tail_rows, self.first
        return [
            (f32(SMALL, C), whole(TAIL_ROWS, C)), (f32(OWN, rows, C), slots(rows)), (f32(OWN, rows, C), slots(rows)),
            (f32(count, OWN, 4, C), copies(count, 4)),
        ]

    def tail_results(self, result):
        self.small, self.du, self.dt, pay = result
        self.back_got = shared(pay, self.stages)

    def tail_backward_steps(self, cotangent, far, back):
        rows = self.tail_rows

        def body(meta, z_ref, r_ref, stat, rstat, gain, bias, means_ref, p_ref, gate_ref, down, down_b, up, up_b, cot_ref, far_ref, back_ref,
                 small, du_out, dt_out, pay, slope_ref):
            m = pl.program_id(0)
            valid = self.valid(meta, m, 4)
            center, spread, rcenter, rspread = stat[0, 0:1], stat[0, 1:2], rstat[0, 0:1], rstat[0, 1:2]
            scale = gain[4:5] * spread
            shift = bias[4:5] - center * scale
            zeros = jnp.zeros((rows - HALF, LANES), F32)
            counts = self.lengths(meta, m)
            ps = [p_ref[0, :, j : j + 1] for j in range(len(counts))]
            gates = [gate_ref[0, j : j + 1, :] for j in range(len(counts))]
            means = [means_ref[0, j : j + 1, :] for j in range(len(counts))]
            res_gain, res_bias, gate_grad = [], [], []
            for cs in CHUNKS:
                u = z_ref[0, :, cs] * scale[:, cs] + shift[:, cs]
                s = sigmoid(u)
                h = valid.keep(u * s)
                slope_ref[:, cs] = valid.keep(s * (1.0 + u * (1.0 - s)))
                rh = (r_ref[0, :, cs] - rcenter[:, cs]) * rspread[:, cs]
                t = h * self.by_segment(gates, cs) + gain[5:6, cs] * rh + bias[5:6, cs]
                s = sigmoid(t)
                here = jnp.where(meta[2 * OWN] == 1, cot_ref[0, 0:HALF, cs], far_ref[0, :, cs])
                cot = jnp.concatenate([here + back_ref[0, :, cs], zeros], axis=0)
                dt = valid.keep(cot * (s * (1.0 + t * (1.0 - s))))
                dt_out[0, :, cs] = dt
                res_bias.append(column_sum(dt))
                res_gain.append(column_sum(dt * rh))
                gate_grad.append(self.seg_sums(dt * h))
            des = [jnp.concatenate([g[j] for g in gate_grad], axis=1) for j in range(len(counts))]
            shares = self.squeeze_back(des, ps, gates, counts, (down, down_b, up, up_b), means, small, m)
            self.last_norm(m, dt_out, du_out, z_ref, slope_ref, gates, shares, center, spread, res_bias, res_gain, pay, small)

        args = [
            (self.z[4], slots(rows)), (self.r, slots(rows)), (self.stats[4], slots(2)), (self.rstat, slots(2)),
            (self.gain, whole(6, C)), (self.bias, whole(6, C)),
            (self.se_state[0], slots(8)), (self.se_state[1], slots(SE, 8)), (self.se_state[2], slots(8)),
        ] + self.se_args() + [(cotangent, slots(HALF)), (far, layer(MB - 1, HALF, C)), (back, slots(HALF))]
        scratch = [pltpu.VMEM((rows, C), F32)]
        result = yield body, self.meta, args, self.tail_outs(), scratch, f"{self.tag}_tail_back", 0, (), ()
        self.tail_results(result)


    def norm_grad(self, du, zh, scale, sums, number, cs):
        return scale[:, cs] * (du - sums[0:1, cs] / number[:, cs] - zh * (sums[1:2, cs] / number[:, cs]))

    def backward_layer(self, i):
        return run(self.backward_steps(i))

    def backward_steps(self, i):
        two, count = self.two, self.first
        strided = i == 4 and not two
        rows = self.rows_of(i)
        n_src = len(self.source_args())

        def body(meta, *refs):
            refs = list(refs)
            take = lambda n: [refs.pop(0) for _ in range(n)]
            m = pl.program_id(0)
            du_ref, z_ref, w_ref, got, n_ref, stat, gain, bias, dw_ref = take(9)
            if i:
                zp_ref, statp = take(2)
            else:
                dxr_ref, = take(1)
                src = take(n_src)
            small, dz_out = take(2)
            if i:
                du_out, pay = take(2)
            elif two:
                back_out, dx_out = take(2)
            else:
                dx_out, = take(1)
            pad, = take(1)
            alt, = take(1) if refs else (None,)
            sums = added(got)
            number = n_ref[0, 1:2, :] if i == 4 else n_ref[0, 0:1, :]
            center, spread = stat[0, 0:1], stat[0, 1:2]
            scale = gain[i : i + 1] * spread
            valid = self.valid(meta, m, i)
            for cs in CHUNKS:
                zh = (z_ref[0, :, cs] - center[:, cs]) * spread[:, cs]
                dz = valid.keep(self.norm_grad(du_ref[0, :, cs], zh, scale, sums, number, cs))
                high, low = halves(dz)
                dz_out[0, :, cs] = high
                dz_out[0, :, C + cs.start : C + cs.stop] = low
            dy = stacked_dot(dz_out[0, :, 0:C], dz_out[0, :, C : 2 * C], w_ref.at[0], True)
            valid_in = self.valid(meta, m, 0)
            if i:
                pcenter, pspread = statp[0, 0:1], statp[0, 1:2]
                pscale = gain[i - 1 : i] * pspread
                pshift = bias[i - 1 : i] - pcenter * pscale
            taps, bias_sum, gain_sum = [[] for _ in range(TAPS)], [], []
            for c, cs in enumerate(CHUNKS):
                grad = dy[:, cs]
                if strided:
                    grad = spread_out(alt.at[c], grad)
                padded = Padded(pad.at[c], two)
                padded.put(grad)
                if i:
                    z = zp_ref[0, :, cs]
                    u = z * pscale[:, cs] + pshift[:, cs]
                    s = sigmoid(u)
                    h = valid_in.keep(u * s)
                else:
                    h = valid_in.keep(self.source(meta, src, cs))
                dh = None
                for k in range(TAPS):
                    moved = padded.get(2 - k)
                    taps[k].append(column_sum(h * moved))
                    term = dw_ref[0, k : k + 1, cs] * moved
                    dh = term if dh is None else dh + term
                if i:
                    du = valid_in.keep(dh * (s * (1.0 + u * (1.0 - s))))
                    du_out[0, :, cs] = du
                    bias_sum.append(column_sum(du))
                    gain_sum.append(column_sum(du * ((z - pcenter[:, cs]) * pspread[:, cs])))
                    continue
                dxr = dxr_ref[0, :, cs]
                if not two:
                    dxr = spread_out(alt.at[c], dxr)
                dx = valid_in.keep(dh) + dxr
                if two:
                    back_out[0, :, cs] = dx[:HALF]
                    dx = dx[HALF:]
                dx_out[0, :, cs] = dx
            rows = taps + [bias_sum, gain_sum] if i else taps
            rows = [jnp.concatenate(x, axis=1) for x in rows]
            for j, row in enumerate(rows):
                accumulate(small, m, j, row)
            if i:
                send(pay, rows[TAPS:])

        sent = 4 if i == 4 else 2
        args = [
            (self.du, slots(rows)), (self.z[i], slots(rows)), self.matrix(i), (self.back_got, copies(self.last, sent)),
            (self.number, slots(2)), (self.stats[i], slots(2)), (self.gain, whole(6, C)), (self.bias, whole(6, C)),
            (self.dw, layer(i, TAPS, C)),
        ]
        if not i:
            args.append((self.dxr, slots(self.tail_rows)))
        args += self.before_args(i)
        place = TAIL_ROWS // 8 + i
        outs = [(f32(SMALL, C), pl.BlockSpec((8, C), lambda m, *_: (place, 0))), (bf16(OWN, rows, 2 * C), slots(rows, 2 * C))]
        if i:
            outs += [(f32(OWN, SLOT, C), slots(SLOT)), (f32(count, OWN, 2, C), copies(count, 2))]
        elif two:
            outs += [(f32(OWN, HALF, C), slots(HALF)), (f32(OWN, HALF, C), slots(HALF))]
        else:
            outs += [(f32(OWN, SLOT, C), slots(SLOT))]
        scratch = [pad_scratch()]
        if strided or (i == 0 and not two):
            scratch.append(stride_scratch())
        flops = 6 * OWN * rows * C * C
        self.small, dz, *result = yield (
            body, self.meta, args, outs, scratch, f"{self.tag}_backward_{i}", flops, self.done, (self.small,)
        )
        got = self.back_got
        if i:
            self.du = result[0]
            if i == self.stop:
                self.pending = dz, result[1]
                return result
            self.back_got = shared(result[1], self.stages)
        self.weight_grad(i, dz)
        if i == 4:
            self.residual_back(got)
        return result

    def residual_back(self, got):
        rows = self.tail_rows

        def body(meta, got, n_ref, dt_ref, r_ref, rstat, gain, w_ref, x_ref, kept_out, away_out, dxr_out, dr, total):
            m = pl.program_id(0)
            sums = added(got)[2:4]
            number = n_ref[0, 1:2, :]
            center, spread = rstat[0, 0:1], rstat[0, 1:2]
            scale = gain[5:6] * spread
            valid = self.valid(meta, m, 4)
            for cs in CHUNKS:
                rh = (r_ref[0, :, cs] - center[:, cs]) * spread[:, cs]
                high, low = halves(valid.keep(self.norm_grad(dt_ref[0, :, cs], rh, scale, sums, number, cs)))
                dr[:, cs] = high
                dr[:, C + cs.start : C + cs.stop] = low
            high, low = dr[:, 0:C], dr[:, C : 2 * C]
            dxr_out[0] = stacked_dot(high, low, w_ref.at[0], True)
            grad = stacked_outer(x_ref[0, :, 0:C], x_ref[0, :, C : 2 * C], high, low)
            self.add_halves(meta, m, grad, total, kept_out, away_out)

        args = [
            (got, copies(self.last, 4)), (self.number, slots(2)), (self.dt, slots(rows)), (self.r, slots(rows)),
            (self.rstat, slots(2)), (self.gain, whole(6, C)), self.matrix(5), (self.picked, slots(rows, 2 * C)),
        ]
        outs = self.piece_out(5) + [(f32(OWN, rows, C), slots(rows))]
        which = PLACES[5][0]
        *self.pieces[which], self.dxr = call(
            body, self.meta, args, outs, [pltpu.VMEM((rows, 2 * C), BF16), pltpu.VMEM((C, C), F32)],
            f"{self.tag}_residual_back", 12 * OWN * rows * C * C, into=self.pieces[which],
        )

    def piece_out(self, i):
        which, place = PLACES[i]
        rows = PIECE_ROWS[which]
        return [(f32(rows, C), pl.BlockSpec((C // 2, C), lambda m, *_: (place, 0)))] * 2

    def add_halves(self, meta, m, grad, total, kept_out, away_out):
        @pl.when(m == 0)
        def _():
            total[...] = grad

        @pl.when(m > 0)
        def _():
            top, bottom = total[0 : C // 2] + grad[0 : C // 2], total[C // 2 : C] + grad[C // 2 : C]
            lower = meta[2 * OWN] == 1
            kept_out[...] = jnp.where(lower, top, bottom)
            away_out[...] = jnp.where(lower, bottom, top)

    def weight_grad(self, i, dz):
        two = self.two
        strided = i == 4 and not two
        rows = self.rows_of(i)
        n_src = len(self.source_args())

        def body(meta, *refs):
            refs = list(refs)
            take = lambda n: [refs.pop(0) for _ in range(n)]
            m = pl.program_id(0)
            if i:
                zp_ref, statp, gain, bias = take(4)
                center, spread = statp[0, 0:1], statp[0, 1:2]
                scale = gain[i - 1 : i] * spread
                shift = bias[i - 1 : i] - center * scale
            else:
                src = take(n_src)
            dz_ref, dw_ref, kept_out, away_out, pad, yh, yl, total = take(8)
            alt, = take(1) if strided else (None,)
            valid_in = self.valid(meta, m, 0)
            for c, cs in enumerate(CHUNKS):
                if i:
                    u = zp_ref[0, :, cs] * scale[:, cs] + shift[:, cs]
                    h = valid_in.keep(u * sigmoid(u))
                else:
                    h = valid_in.keep(self.source(meta, src, cs))
                padded = Padded(pad.at[c], two)
                padded.put(h)
                y = padded.conv(dw_ref[0, :, cs])
                if strided:
                    y = every_other(alt.at[c], y)
                yh[:, cs], yl[:, cs] = halves(y)
            grad = stacked_outer(yh[...], yl[...], dz_ref[0, :, 0:C], dz_ref[0, :, C : 2 * C])
            self.add_halves(meta, m, grad, total, kept_out, away_out)

        args = self.before_args(i)
        if i:
            args += [(self.gain, whole(6, C)), (self.bias, whole(6, C))]
        args += [(dz, slots(rows, 2 * C)), (self.dw, layer(i, TAPS, C))]
        scratch = [pad_scratch(), pltpu.VMEM((rows, C), BF16), pltpu.VMEM((rows, C), BF16), pltpu.VMEM((C, C), F32)]
        if strided:
            scratch.append(stride_scratch())
        which = PLACES[i][0]
        self.pieces[which] = call(
            body, self.meta, args, self.piece_out(i), scratch, f"{self.tag}_weights_{i}", 6 * OWN * rows * C * C,
            into=self.pieces[which],
        )
        self.done = (self.pieces[which][0],)

    def backward(self, layers):
        if layers[0] == 4:
            self.pieces = [[], []]
        for i in layers:
            result = self.backward_layer(i)
        return result

    def resume(self, i):
        dz, payload = self.pending
        self.back_got = shared(payload, self.stages)
        self.weight_grad(i, dz)

    def fork(self, state=None):
        other = copy.copy(self)
        other.__dict__.update(state or {})
        if "pieces" in other.__dict__:
            other.pieces = list(other.pieces)
        return other

    def state(self):
        return {name: getattr(self, name) for name in ("du", "dxr", "pieces", "small", "pending")}

    def half(self, no, first, begin=None, end=None):
        kept, away = self.pieces[no]
        if no:
            parts = self.small[: SMALL // 2], self.small[SMALL // 2 :]
            at = kept.shape[0] - SMALL // 2
            kept = lax.dynamic_update_slice_in_dim(kept, jnp.where(first, *parts), at, 0)
            away = lax.dynamic_update_slice_in_dim(away, jnp.where(first, *parts[::-1]), at, 0)
        if begin is not None:
            away, _ = lax.optimization_barrier((away, begin))
            kept, _ = lax.optimization_barrier((kept, end))
        return kept + swap(away)


PLACES = {3: (0, 0), 4: (0, 1), 5: (0, 2), 0: (1, 0), 1: (1, 1), 2: (1, 2)}
PIECE_ROWS = (3 * C // 2, 3 * C // 2 + SMALL // 2)


def split_squeeze(meta, own, far):
    def body(meta, own_ref, far_ref, *outs):
        row, col = (lax.broadcasted_iota(jnp.int32, (SE, C), axis) for axis in (0, 1))
        for block in range(2):
            down, down_b, up, up_b = outs[4 * block : 4 * block + 4]
            down[...] = choose(meta, block, own_ref[0:SE, :], far_ref[0:SE, :])
            up[...] = choose(meta, block, own_ref[SE : 2 * SE, :], far_ref[SE : 2 * SE, :])
            up_b[...] = choose(meta, block, own_ref[2 * SE : 2 * SE + 1, :], far_ref[2 * SE : 2 * SE + 1, :])
            wide = choose(meta, block, own_ref[2 * SE + 1 : 2 * SE + 2, :], far_ref[2 * SE + 1 : 2 * SE + 2, :])
            down_b[...] = jnp.sum(jnp.where(row == col, wide, 0.0), axis=1, keepdims=True)

    shapes = [(SE, C), (SE, 1), (SE, C), (1, C)] * 2
    args = [(x, whole(*x.shape)) for x in (own, far)]
    outs = call(body, meta, args, [(f32(*shape), whole(*shape)) for shape in shapes], name="split_squeeze", steps=1)
    return tuple(outs[:4]), tuple(outs[4:])


def pick_joining(picks, features):
    def body(picks, in_ref, out_ref):
        out_ref[...] = in_ref[0, 0]

    own = pl.BlockSpec((1, 1, HALF, C), lambda m, picks: (picks[m], 1, 0, 0))
    out = (f32(OWN * HALF, C), pl.BlockSpec((HALF, C), lambda m, *_: (m, 0)))
    return call(body, picks, [(features, own)], [out], name="pick_joining")[0]


def swap(x):
    return lax.ppermute(x, "section", [(0, 1), (1, 0)])


def fenced(always, work, x):
    shapes = jax.eval_shape(work, x)
    return lax.cond(always, work, lambda x: jax.tree.map(lambda y: jnp.zeros(y.shape, y.dtype), shapes), x)


class Reduction:
    def __init__(self, x, stages):
        self.x = x
        self.todo = []
        stride = 1
        for radix in stages:
            self.todo.append((True, radix, stride))
            stride *= radix
        self.todo += [(False, radix, stride) for _, radix, stride in reversed(self.todo)]

    def step(self):
        scatter, radix, stride = self.todo.pop(0)
        rows = self.x.shape[0]
        if scatter:
            parts = exchange(self.x.reshape(radix, rows // radix, C), radix, stride)
            self.x = jnp.sum(parts, axis=0)
        else:
            parts = exchange(jnp.broadcast_to(self.x, (radix,) + self.x.shape), radix, stride)
            self.x = parts.reshape(radix * rows, C)
        return (self.x,)

    def finish(self):
        while self.todo:
            self.step()
        return self.x


def per_device(features, out_grad, lengths, join_pick, dw, pw, gain, bias, res_w, down, down_b, up, up_b):
    first = lax.axis_index("section") == 0
    size = lax.axis_size("dp")
    inputs = features.reshape(MB, SLOT, C)
    cotangent = out_grad.reshape(MB, SLOT, C)
    own, picks = lengths[0, 0], join_pick[0]
    to_upper = lambda x: lax.ppermute(x, "section", [(0, 1)])
    to_lower = lambda x: lax.ppermute(x, "section", [(1, 0)])

    far_len = swap(own)
    far_rows = to_upper(inputs[MB - 1])
    far_w0 = swap(pw[0, 0:1])
    taps = jnp.concatenate([dw[0].reshape(5 * TAPS, C), gain[0], bias[0]], axis=0)
    far_taps = swap(taps)
    far_pw, far_res = swap(pw[0]), swap(res_w[0])
    wide = jnp.pad(down_b, ((0, 0), (0, C - SE)))
    squeeze = jnp.concatenate([down[0].T, up[0], up_b, wide], axis=0)
    far_squeeze = swap(squeeze)
    far_cot = swap(cotangent)

    flag = first.astype(jnp.int32)[None]
    mine = lambda v: jnp.where(first, v[:OWN], jnp.concatenate([v[OWN:], jnp.zeros((1,), v.dtype)]))
    length = mine(jnp.where(first, own, far_len))
    half_len = (length + 1) // 2
    join_len = mine(jnp.where(first, far_len, own)[picks])
    meta1 = jnp.concatenate([length, half_len, flag])
    meta2 = jnp.concatenate([half_len, join_len, flag, picks[MB - 1 :]])
    both = jnp.concatenate([length, half_len, flag, half_len, join_len, flag, picks[MB - 1 :]])

    def small(block):
        t = jnp.where(first == (block == 0), taps, far_taps)
        return t[: 5 * TAPS].reshape(5, TAPS, C), t[5 * TAPS : 5 * TAPS + 6], t[5 * TAPS + 6 :]

    excitations = split_squeeze(meta1, squeeze, far_squeeze)

    def prepared(block, start, stop):
        array = prepare(meta1, (pw[0], res_w[0]), (far_pw, far_res), block, start, stop)
        return array, {i: (array, i - start) for i in range(start, stop)}

    parts0 = [prepared(0, 1, 3), prepared(0, 3, 6)]
    parts1 = [prepared(1, 0, 1), prepared(1, 1, 4), prepared(1, 4, 6)]

    stages, deep = radices(size, 16), radices(size, 4)
    c14 = Block(False, meta1, small(0), {**parts0[0][1], **parts0[1][1]}, stages)
    c14.x, c14.x_far, c14.first_matrix = inputs, far_rows, (pw[0], far_w0)
    c14.excitation = excitations[0]
    c14.forward({2: (parts0[1][0],)})
    late_picks, _ = lax.optimization_barrier((picks, c14.z[3]))
    far_joining = to_lower(pick_joining(late_picks, features.reshape(MB, 2, HALF, C)))
    c15 = Block(True, meta2, small(1), {**parts1[0][1], **parts1[1][1], **parts1[2][1]}, stages)
    c15.excitation = excitations[1]
    c15.arrived, c15.joined_far, c15.joined = Linked(0, HALF), far_joining, features.reshape(MB, 2, HALF, C)
    c15.start()
    out0, _ = run_joined(c14.tail_steps(), c15.forward_steps(0), (both, 0, meta1.shape[0]))
    c15.arrived = out0
    c15.forward({1: (parts1[1][0],), 2: (parts1[2][0],)}, joined=True)
    out1 = c15.tail(cotangent, far_cot)
    c15.stop = 2
    c15.backward((4, 3))
    begin = c15.back_got
    c15.backward((2,))
    always = own[0] > 0

    half0 = c15.half(0, first, begin, c15.du)
    sum0 = lax.psum(half0, "dp")

    def middle(half0):
        upper, lower = c15.fork(), c14.fork()
        upper.resume(2)
        upper.done += (half0,)
        upper.backward((1,))
        (_, dx1), _ = run_joined(
            upper.backward_steps(0), lower.tail_backward_steps(cotangent, far_cot, Linked(2, HALF)), (both, meta1.shape[0], 0)
        )
        lower.done = upper.done
        lower.backward((4,))
        begin1 = lower.back_got
        lower.backward((3,))
        half1 = upper.half(1, first, begin1, lower.du)
        begin2 = lower.back_got
        lower.stop = 2
        lower.backward((2,))
        half2 = lower.half(0, first, begin2, lower.du)
        return dx1, jnp.concatenate([half1, half2], axis=0), lower.state()

    dx1, half12, state = fenced(always, middle, half0)
    sum0, half12 = lax.optimization_barrier((sum0, half12))
    sum12 = lax.psum(half12, "dp")

    def ending(half12):
        last = c14.fork(state)
        last.resume(2)
        last.done += (half12,)
        came0 = to_upper(sum0)
        dx0, = last.backward((1, 0))
        half3 = last.half(1, first)
        half3, dx0, *kept = lax.optimization_barrier((half3, dx0, out0, out1, dx1))
        reduction = Reduction(half3, deep)
        reduction.step()
        pad = jnp.zeros((1, HALF, C), F32)
        lower = jnp.concatenate([kept[0], jnp.concatenate([to_lower(kept[0][0:1, :HALF]), pad], axis=1)], axis=0)
        upper = jnp.concatenate([to_upper(kept[1]), kept[1][0:1]], axis=0)
        block_out = jnp.where(first, lower, upper)
        lower = jnp.concatenate([dx0, to_lower(dx0[0:1])], axis=0)
        joins = jnp.concatenate([to_upper(kept[2]), kept[2][0:1]], axis=0)
        joins = jnp.stack([lax.dynamic_index_in_dim(joins, jnp.argmax(picks == s), 0, False) for s in range(MB)])
        upper = jnp.concatenate([jnp.zeros_like(joins), joins], axis=1)
        dx = jnp.where(first, lower, upper)
        reduction.x, block_out, dx, came0 = lax.optimization_barrier((reduction.x, block_out, dx, came0))
        return block_out, dx, came0, reduction.finish()

    block_out, dx, came0, sum3 = fenced(always, ending, half12)
    came3 = to_lower(sum3)
    sum12, _ = lax.optimization_barrier((sum12, sum3))
    came12 = swap(sum12)
    split = PIECE_ROWS[1]
    sum1, sum2, came1, came2 = sum12[:split], sum12[split:], came12[:split], came12[split:]

    lead = 3 * C // 2

    def joined(near, far):
        pair = [x.reshape(-1, 1, C // 2, C) for x in (near, far)]
        both = jnp.where(first, jnp.concatenate(pair, axis=1), jnp.concatenate(pair[::-1], axis=1))
        return both.reshape(-1, C, C)

    choose_mine = lambda a, b: jnp.where(first, a, b)
    rest_part = joined(choose_mine(sum3[:lead], sum1[:lead]), choose_mine(came3[:lead], came1[:lead]))
    lead_part = joined(choose_mine(sum2[:C], sum0[:C]), choose_mine(came2[:C], came0[:C]))
    pw_grad = jnp.concatenate([rest_part, lead_part], axis=0)[None]
    res_grad = joined(choose_mine(sum2[C:], sum0[C:]), choose_mine(came2[C:], came0[C:]))
    near, far = choose_mine(sum3[lead:], sum1[lead:]), choose_mine(came3[lead:], came1[lead:])
    rows = jnp.where(first, jnp.concatenate([near, far], axis=0), jnp.concatenate([far, near], axis=0))
    dw_grad = rows[TAIL_ROWS : TAIL_ROWS + 40].reshape(1, 5, 8, C)
    norms = jnp.concatenate([dw_grad[0, 1:, TAPS : TAPS + 2], rows[None, 2 * SE + 2 : 2 * SE + 4], rows[None, 2 * SE + 4 : 2 * SE + 6]], axis=0)
    return (
        block_out.reshape(features.shape), dx.reshape(features.shape), dw_grad[:, :, :TAPS], pw_grad,
        norms[None, :, 1], norms[None, :, 0], res_grad, rows[SE : 2 * SE].T[None], rows[2 * SE + 1 : 2 * SE + 2, :SE],
        rows[:SE][None], rows[2 * SE : 2 * SE + 1],
    )


def solution(mesh):
    rows = P("section", "dp", None)
    own = lambda dims: P("section", *([None] * dims))
    weights = (own(3), own(3), own(2), own(2), own(2), own(2), own(1), own(2), own(1))
    in_specs = (rows, rows, rows, P("dp", None), *weights)
    out_specs = (rows, rows, *weights)
    return jax.shard_map(per_device, mesh=mesh, in_specs=in_specs, out_specs=out_specs, check_vma=False)
```

profile of v0, /device:TPU:0, one launch (start us, length us, event | category | flops | bytes accessed | tf_op | source)
XLA Modules:
  0.0 631.6 jit_solution(3116461479992217824)
XLA Ops:
  20.3 5.6 c14_forward_0.1
  25.9 7.9 %all-to-all-start.11 = ((f32[16,2,2,640]{3,2,1,0:T(2,128)}), f32[16,2,2,640]{3,2,1,0:T(2,128)}, u32[]{:S(2)}, u32[]{:S(2)}) async-start(f32[16,2,2,640]{3,2,1,0:T(2,128)} %get-tuple-element.398), calls=%async_computation.11 | async-start | bytes 327680 | tf_op jit(solution)/shard_map/all_to_all | solution.py:42
  42.2 5.9 c14_forward_1.1
  60.1 5.9 c14_forward_2.1
  78.9 5.9 c14_forward_3.1
  116.3 6.9 %c14_tail_c15_forward_0.1 = (f32[2,400,512]{2,1,0:T(8,128)}, f32[2,2,512]{2,1,0:T(2,128)}, f32[2,2,512]{2,1,0:T(2,128)}, f32[2,8,512]{2,1,0:T(8,128)}, f32[2,64,...) custom-call(s32[11]{0:T(128)S(1)} %concatenate.83.meta, ...), custom_call_target="tpu_custom_call" | custom-call | flops 1258291200 | bytes 10297600 | tf_op jit(solution)/shard_map/c14_tail_c15_forward_0/pallas_call | solution.py:211
  123.2 7.1 %all-to-all-start.16 = ((f32[16,2,2,640]{3,2,1,0:T(2,128)}), f32[16,2,2,640]{3,2,1,0:T(2,128)}, u32[]{:S(2)}, u32[]{:S(2)}) async-start(f32[16,2,2,640]{3,2,1,0:T(2,128)} %get-tuple-element.416), calls=%async_computation.16 | async-start | bytes 327680 | tf_op jit(solution)/shard_map/all_to_all | solution.py:42
  131.8 6.0 prepare_1_1.1.refs_5_.refs_6_.refs_7_.refs_2_
  138.2 5.8 c15_forward_1.1
  144.1 6.6 %all-to-all-start.17 = ((f32[16,2,2,512]{3,2,1,0:T(2,128)}), f32[16,2,2,512]{3,2,1,0:T(2,128)}, u32[]{:S(2)}, u32[]{:S(2)}) async-start(f32[16,2,2,512]{3,2,1,0:T(2,128)} %get-tuple-element.418), calls=%async_computation.17 | async-start | bytes 262144 | tf_op jit(solution)/shard_map/all_to_all | solution.py:42
  158.5 5.8 c15_forward_2.1
  176.4 5.8 c15_forward_3.1
  182.2 12.7 %all_to_all.111.refs_1_.refs_3_ = f32[16,2,4,512]{3,2,1,0:T(4,128)} all-to-all(f32[16,2,4,512]{3,2,1,0:T(4,128)} %get-tuple-element.425), channel_id=1, replica_groups=mesh['section'=2,'dp'=16] {'dp'}, dimensions={0} | all-to-all | bytes 524288 | tf_op jit(solution)/shard_map/all_to_all | solution.py:42
  194.9 5.8 c15_forward_4.1
  204.2 7.8 %all-to-all-done.20.refs_1_ = f32[16,2,2,512]{3,2,1,0:T(2,128)S(1)} async-done(((f32[16,2,2,512]{3,2,1,0:T(2,128)}), f32[16,2,2,512]{3,2,1,0:T(2,128)S(1)}, u32[]{:S(2)}, u32[]{:S(2)}) %all-to-all-start.20) | async-done | bytes 131104 | tf_op jit(solution)/shard_map/all_to_all | solution.py:42
  212.7 8.7 %c15_tail.1 = (f32[2,400,512]{2,1,0:T(8,128)}, f32[2,2,512]{2,1,0:T(2,128)}, f32[2,2,512]{2,1,0:T(2,128)}, f32[2,8,512]{2,1,0:T(8,128)}, f32[2,64,8]{2,1,0:T(8,1...) custom-call(s32[6]{0:T(128)S(1)} %pad_add_fusion.2.meta, ...), custom_call_target="tpu_custom_call" | custom-call | bytes 14670080 | tf_op jit(solution)/shard_map/c15_tail/pallas_call | solution.py:211
  221.3 12.7 %all_to_all.112.refs_3_.refs_0_ = f32[16,2,4,512]{3,2,1,0:T(4,128)} all-to-all(f32[16,2,4,512]{3,2,1,0:T(4,128)} %get-tuple-element.434), channel_id=1, replica_groups=mesh['section'=2,'dp'=16] {'dp'}, dimensions={0} | all-to-all | bytes 524288 | tf_op jit(solution)/shard_map/all_to_all | solution.py:42
  234.0 7.9 %c15_backward_4.1 = (f32[256,512]{1,0:T(8,128)S(1)}, bf16[2,400,1024]{2,1,0:T(8,128)(2,1)}, f32[2,400,512]{2,1,0:T(8,128)}, f32[16,2,2,512]{3,2,1,0:T(2,128)}) custom-call(s32[6]{0:T(128)S(1)} %pad_add_fusion.2.meta, f32[2,400,512]{2,1,0:T(8,128)} %get-tuple-element.433.refs_0_, ...), custom_call_target="tpu_custom_call", output_to_operand_aliasing={{0}: (12, {})} | custom-call | flops 1258291200 | bytes 11307008 | tf_op jit(solution)/shard_map/c15_backward_4/pallas_call | solution.py:211
  245.7 6.1 c15_weights_4.1
  254.1 7.7 %c15_backward_3.1 = (f32[256,512]{1,0:T(8,128)S(1)}, bf16[2,400,1024]{2,1,0:T(8,128)(2,1)}, f32[2,400,512]{2,1,0:T(8,128)}, f32[16,2,2,512]{3,2,1,0:T(2,128)}) custom-call(s32[6]{0:T(128)S(1)} %pad_add_fusion.2.meta, f32[2,400,512]{2,1,0:T(8,128)} %get-tuple-element.438.refs_0_, ...), custom_call_target="tpu_custom_call", output_to_operand_aliasing={{0}: (13, {})} | custom-call | flops 1258291200 | bytes 12224512 | tf_op jit(solution)/shard_map/c15_backward_3/pallas_call | solution.py:211
  267.3 7.6 %c15_residual_back.1 = (f32[768,512]{1,0:T(8,128)}, f32[768,512]{1,0:T(8,128)}, f32[2,400,512]{2,1,0:T(8,128)}) custom-call(s32[6]{0:T(128)S(1)} %pad_add_fusion.2.meta, f32[16,2,4,512]{3,2,1,0:T(4,128)} %all_to_all.112.refs_3_.refs_0_, f32[2,2,512]{2,1,0:T(2,128)S(1)} %get-tuple-element.419.refs_2_.refs_4_.refs_1_, ...), custom_call_target="tpu_custom_call", output_to_operand_aliasing={{0}: (9, {}), {1}: (10, {})} | custom-call | flops 2516582400 | bytes 12087296 | tf_op jit(solution)/shard_map/c15_residual_back/pallas_call | solution.py:211
  274.9 6.0 c15_weights_3.1
  281.6 8.3 %c15_backward_2.1 = (f32[256,512]{1,0:T(8,128)}, bf16[2,400,1024]{2,1,0:T(8,128)(2,1)}, f32[2,400,512]{2,1,0:T(8,128)}, f32[16,2,2,512]{3,2,1,0:T(2,128)}) custom-call(s32[6]{0:T(128)} %copy-done.48, f32[2,400,512]{2,1,0:T(8,128)} %get-tuple-element.444.refs_0_, ...), custom_call_target="tpu_custom_call", output_to_operand_aliasing={{0}: (13, {})} | custom-call | flops 1258291200 | bytes 12224512 | tf_op jit(solution)/shard_map/c15_backward_2/pallas_call | solution.py:211
  293.5 122.5 %conditional.2 = (f32[2,200,512]{2,1,0:T(8,128)}, f32[1664,512]{1,0:T(8,128)}, f32[2,400,512]{2,1,0:T(8,128)}, f32[2,208,512]{2,1,0:T(8,128)}, bf16[2,400,1024]{...) conditional(s32[]{:T(128)} %bitcast.6, () %tuple.46, (f32[16,2,2,512]{3,2,1,0:T(2,128)}, ...), branch_computations={%region_0.1_spmd, %region_1.2_spmd} | conditional | flops 12685410304 | bytes 178855648 | solution.py:1020
  293.6 7.3 %all-to-all-start = ((f32[16,2,2,512]{3,2,1,0:T(2,128)}), f32[16,2,2,512]{3,2,1,0:T(2,128)S(1)}, u32[]{:S(2)}, u32[]{:S(2)}) async-start(f32[16,2,2,512]{3,2,1,0:T(2,128)} %get-tuple-element.157), calls=%async_computation | async-start | bytes 262144 | tf_op jit(solution)/shard_map/cond/branch_1_fun/all_to_all | solution.py:42
  301.0 6.7 %c15_weights_2.1 = (f32[896,512]{1,0:T(8,128)}, f32[896,512]{1,0:T(8,128)}) custom-call(s32[6]{0:T(128)} %get-tuple-element.153.meta, f32[2,400,512]{2,1,0:T(8,128)} %get-tuple-element.155.refs_0_.refs_1_, f32[2,2,512]{2,1,0:T(2,128)} %get-tuple-element.159.refs_1_.refs_5_, f32[6,512]{1,0:T(8,128)} %get-tuple-element.160.refs_2_.refs_6_, ...), custom_call_target="tpu_custom_call" | custom-call | flops 1258291200 | bytes 7030784 | tf_op jit(solution)/shard_map/cond/branch_1_fun/c15_weights_2/pallas_call | solution.py:211
  311.9 8.1 %c15_backward_1.1 = (f32[256,512]{1,0:T(8,128)S(1)}, bf16[2,400,1024]{2,1,0:T(8,128)(2,1)}, f32[2,400,512]{2,1,0:T(8,128)}, f32[16,2,2,512]{3,2,1,0:T(2,128)}) custom-call(s32[6]{0:T(128)S(1)} %copy-done.49, f32[2,400,512]{2,1,0:T(8,128)} %get-tuple-element.154.refs_0_, ...), custom_call_target="tpu_custom_call", output_to_operand_aliasing={{0}: (14, {})} | custom-call | flops 1258291200 | bytes 12224512 | tf_op jit(solution)/shard_map/cond/branch_1_fun/c15_backward_1/pallas_call | solution.py:211
  324.5 6.0 c15_weights_1.1
  333.0 9.5 %c15_backward_0_c14_tail_back.1 = (f32[256,512]{1,0:T(8,128)S(1)}, bf16[2,400,1024]{2,1,0:T(8,128)(2,1)}, f32[2,200,512]{2,1,0:T(8,128)}, f32[2,200,512]{2,1,0:T...) custom-call(s32[11]{0:T(128)} %get-tuple-element.152.meta, ...), custom_call_target="tpu_custom_call", output_to_operand_aliasing={{0}: (30, {})} | custom-call | flops 1258291200 | bytes 24387840 | tf_op jit(solution)/shard_map/cond/branch_1_fun/c15_backward_0_c14_tail_back/pallas_call | solution.py:211
  347.7 5.7 c15_weights_0.1
  356.4 7.1 %c14_backward_4.1 = (f32[256,512]{1,0:T(8,128)S(1)}, bf16[2,208,1024]{2,1,0:T(8,128)(2,1)}, f32[2,400,512]{2,1,0:T(8,128)}, f32[16,2,2,512]{3,2,1,0:T(2,128)}) custom-call(s32[5]{0:T(128)S(1)} %copy-done.44, f32[2,208,512]{2,1,0:T(8,128)} %get-tuple-element.202.refs_0_, ...), custom_call_target="tpu_custom_call", output_to_operand_aliasing={{0}: (13, {})} | custom-call | flops 654311424 | bytes 9996288 | tf_op jit(solution)/shard_map/cond/branch_1_fun/c14_backward_4/pallas_call | solution.py:211
  367.9 5.6 c14_weights_4.1
  375.8 7.7 %c14_backward_3.1 = (f32[256,512]{1,0:T(8,128)S(1)}, bf16[2,400,1024]{2,1,0:T(8,128)(2,1)}, f32[2,400,512]{2,1,0:T(8,128)}, f32[16,2,2,512]{3,2,1,0:T(2,128)}) custom-call(s32[5]{0:T(128)S(1)} %copy-done.44, f32[2,400,512]{2,1,0:T(8,128)} %get-tuple-element.210.refs_0_, ...), custom_call_target="tpu_custom_call", output_to_operand_aliasing={{0}: (13, {})} | custom-call | flops 1258291200 | bytes 12224512 | tf_op jit(solution)/shard_map/cond/branch_1_fun/c14_backward_3/pallas_call | solution.py:211
  383.5 5.6 all-to-all-start.4
  389.1 6.3 c14_residual_back.1
  395.4 5.9 c14_weights_3.1
  401.6 8.2 %c14_backward_2.1 = (f32[256,512]{1,0:T(8,128)}, bf16[2,400,1024]{2,1,0:T(8,128)(2,1)}, f32[2,400,512]{2,1,0:T(8,128)}, f32[16,2,2,512]{3,2,1,0:T(2,128)}) custom-call(s32[5]{0:T(128)} %get-tuple-element.201.meta, f32[2,400,512]{2,1,0:T(8,128)} %get-tuple-element.217.refs_0_, ...), custom_call_target="tpu_custom_call", output_to_operand_aliasing={{0}: (13, {})} | custom-call | flops 1258291200 | bytes 11175936 | tf_op jit(solution)/shard_map/cond/branch_1_fun/c14_backward_2/pallas_call | solution.py:211
  416.9 177.3 %conditional.3 = (f32[768,512]{1,0:T(8,128)}, f32[896,512]{1,0:T(8,128)}, f32[1,1200,512]{2,1,0:T(8,128)}, f32[1,1200,512]{2,1,0:T(8,128)}, f32[512,512]{1,0:T(8...) conditional(s32[]{:T(128)} %bitcast.6, () %tuple.45, ...), branch_computations={%region_3.4_spmd, %region_4.10_spmd} | conditional | flops 6300770304 | bytes 142101728 | solution.py:1020
  416.9 6.7 %all-to-all-start.5 = ((f32[16,2,2,512]{3,2,1,0:T(2,128)}), f32[16,2,2,512]{3,2,1,0:T(2,128)S(1)}, u32[]{:S(2)}, u32[]{:S(2)}) async-start(f32[16,2,2,512]{3,2,1,0:T(2,128)} %get-tuple-element.247), calls=%async_computation.5 | async-start | bytes 262144 | tf_op jit(solution)/shard_map/cond/branch_1_fun/all_to_all | solution.py:42
  423.6 6.1 c14_weights_2.1
  432.4 8.0 %c14_backward_1.1 = (f32[256,512]{1,0:T(8,128)S(1)}, bf16[2,400,1024]{2,1,0:T(8,128)(2,1)}, f32[2,400,512]{2,1,0:T(8,128)}, f32[16,2,2,512]{3,2,1,0:T(2,128)}) custom-call(s32[5]{0:T(128)S(1)} %get-tuple-element.241.meta, f32[2,400,512]{2,1,0:T(8,128)} %get-tuple-element.244.refs_0_, ...), custom_call_target="tpu_custom_call", output_to_operand_aliasing={{0}: (14, {})} | custom-call | flops 1258291200 | bytes 11175936 | tf_op jit(solution)/shard_map/cond/branch_1_fun/c14_backward_1/pallas_call | solution.py:211
  445.3 6.1 c14_weights_1.1
  456.4 7.4 %c14_backward_0.1 = (f32[256,512]{1,0:T(8,128)S(1)}, bf16[2,400,1024]{2,1,0:T(8,128)(2,1)}, f32[2,400,512]{2,1,0:T(8,128)}) custom-call(s32[5]{0:T(128)S(1)} %get-tuple-element.241.meta, f32[2,400,512]{2,1,0:T(8,128)} %get-tuple-element.259.refs_0_, f32[2,400,512]{2,1,0:T(8,128)} %get-tuple-element.253.refs_9_.refs_0_.refs_1_, ...), custom_call_target="tpu_custom_call", output_to_operand_aliasing={{0}: (14, {})} | custom-call | flops 1258291200 | bytes 12478464 | tf_op jit(solution)/shard_map/cond/branch_1_fun/c14_backward_0/pallas_call | solution.py:211
  463.8 5.6 c14_weights_0.1
  514.8 19.6 %all_to_all.109 = f32[4,56,512]{2,1,0:T(8,128)S(1)} all-to-all(f32[4,56,512]{2,1,0:T(8,128)S(1)} %bitcast.94), channel_id=1, replica_groups={{0,4,8,12},{1,5,9,13},{2,6,10,14},{3,7,11,15},{16,20,24,28},{17,21,25,2..., dimensions={0} | all-to-all | bytes 917504 | tf_op jit(solution)/shard_map/cond/branch_1_fun/all_to_all | solution.py:47
  534.5 21.7 %all_to_all.110 = f32[4,56,512]{2,1,0:T(8,128)S(1)} all-to-all(f32[4,56,512]{2,1,0:T(8,128)S(1)} %broadcast_in_dim.19), channel_id=1, replica_groups={{0,4,8,12},{1,5,9,13},{2,6,10,14},{3,7,11,15},{16,20,24,28},{17,21,25,2..., dimensions={0} | all-to-all | bytes 917504 | tf_op jit(solution)/shard_map/cond/branch_1_fun/all_to_all | solution.py:47
  565.7 25.7 %all-to-all-done.10 = f32[4,224,512]{2,1,0:T(8,128)} async-done(((f32[4,224,512]{2,1,0:T(8,128)}), f32[4,224,512]{2,1,0:T(8,128)}, u32[]{:S(2)}, u32[]{:S(2)}) %all-to-all-start.10) | async-done | bytes 1835040 | tf_op jit(solution)/shard_map/cond/branch_1_fun/all_to_all | solution.py:47
  594.2 11.7 %all-reduce.8.cloned.1.call-done = f32[1664,512]{1,0:T(8,128)} async-done(((f32[1664,512]{1,0:T(8,128)}), f32[1664,512]{1,0:T(8,128)}) %all-reduce.8.cloned.1.call-update) | async-done | bytes 3407888 | tf_op jit(solution)/shard_map/psum | solution.py:1137
  (297 shorter events, 234.0 us)
Async XLA Ops:
  7.2 26.7 %collective-permute-start.12 = (f32[5,512,512]{2,1,0:T(8,128)}, f32[5,512,512]{2,1,0:T(8,128)}, u32[]{:S(2)}, u32[]{:S(2)}) collective-permute-start(f32[5,512,512]{2,1,0:T(8,128)} %bitcast.74), channel_id=1, source_target_pairs={{0,16},{16,0},{1,17},{17,1},{2,18},{18,2},{3,19},{19,3},{4,20},{20... | collective-permute-start | bytes 15728648 | tf_op jit(solution)/shard_map/ppermute | solution.py:1015
  7.7 7.8 %collective-permute-start.8 = (s32[3]{0:T(128)}, s32[3]{0:T(128)S(1)}, u32[]{:S(2)}, u32[]{:S(2)}) collective-permute-start(s32[3]{0:T(128)} %bitcast.100), channel_id=1, source_target_pairs={{0,16},{16,0},{1,17},{17,1},{2,18},{18,2},{3,19},{19,3},{4,20},{20... | collective-permute-start | bytes 44 | tf_op jit(solution)/shard_map/ppermute | solution.py:1015
  9.9 10.3 %collective-permute-start.9 = (f32[400,512]{1,0:T(8,128)}, f32[400,512]{1,0:T(8,128)S(1)}, u32[]{:S(2)}, u32[]{:S(2)}) collective-permute-start(f32[400,512]{1,0:T(8,128)} %slice_bitcast_fusion.1), channel_id=1, source_target_pairs={{0,16},{1,17},{2,18},{3,19},{4,20},{5,21},{6,22},{7,23},{8,24},{9,... | collective-permute-start | bytes 2457608 | tf_op jit(solution)/shard_map/ppermute | solution.py:1056
  14.7 5.6 collective-permute-start.11
  14.9 3.8 collective-permute-start.10
  15.5 36.1 %collective-permute-start.13 = (f32[512,512]{1,0:T(8,128)}, f32[512,512]{1,0:T(8,128)}, u32[]{:S(2)}, u32[]{:S(2)}) collective-permute-start(f32[512,512]{1,0:T(8,128)} %bitcast.89), channel_id=1, source_target_pairs={{0,16},{16,0},{1,17},{17,1},{2,18},{18,2},{3,19},{19,3},{4,20},{20... | collective-permute-start | bytes 3145736 | tf_op jit(solution)/shard_map/ppermute | solution.py:1015
  16.9 92.6 %copy-start.55 = (s32[2]{0:T(128)}, s32[2]{0:T(128)S(1)}, u32[]{:S(2)}) copy-start(s32[2]{0:T(128)S(1)} %get-tuple-element.527) | copy-start | bytes 28
  25.9 16.4 %all-to-all-start.11 = ((f32[16,2,2,640]{3,2,1,0:T(2,128)}), f32[16,2,2,640]{3,2,1,0:T(2,128)}, u32[]{:S(2)}, u32[]{:S(2)}) async-start(f32[16,2,2,640]{3,2,1,0:T(2,128)} %get-tuple-element.398), calls=%async_computation.11 | async-start | bytes 327680 | tf_op jit(solution)/shard_map/all_to_all | solution.py:42
  33.8 82.4 %copy-start.17 = (f32[6,512]{1,0:T(8,128)}, f32[6,512]{1,0:T(8,128)S(1)}, u32[]{:S(2)}) copy-start(f32[6,512]{1,0:T(8,128)S(1)} %get-tuple-element.544.refs_3_.refs_4_.refs_6_) | copy-start | bytes 36868
  48.1 11.3 %all-to-all-start.12 = ((f32[16,2,2,512]{3,2,1,0:T(2,128)}), f32[16,2,2,512]{3,2,1,0:T(2,128)S(1)}, u32[]{:S(2)}, u32[]{:S(2)}) async-start(f32[16,2,2,512]{3,2,1,0:T(2,128)} %get-tuple-element.400), calls=%async_computation.12 | async-start | bytes 262144 | tf_op jit(solution)/shard_map/all_to_all | solution.py:42
  66.0 12.2 %all-to-all-start.13 = ((f32[16,2,2,512]{3,2,1,0:T(2,128)}), f32[16,2,2,512]{3,2,1,0:T(2,128)S(1)}, u32[]{:S(2)}, u32[]{:S(2)}) async-start(f32[16,2,2,512]{3,2,1,0:T(2,128)} %get-tuple-element.403), calls=%async_computation.13 | async-start | bytes 262144 | tf_op jit(solution)/shard_map/all_to_all | solution.py:42
  84.8 12.9 %all-to-all-start.14 = ((f32[16,2,4,512]{3,2,1,0:T(4,128)}), f32[16,2,4,512]{3,2,1,0:T(4,128)}, u32[]{:S(2)}, u32[]{:S(2)}) async-start(f32[16,2,4,512]{3,2,1,0:T(4,128)} %get-tuple-element.406), calls=%async_computation.14 | async-start | bytes 524288 | tf_op jit(solution)/shard_map/all_to_all | solution.py:42
  90.6 25.6 %collective-permute-start.15 = (f32[400,512]{1,0:T(8,128)}, f32[400,512]{1,0:T(8,128)S(1)}, u32[]{:S(2)}, u32[]{:S(2)}) collective-permute-start(f32[400,512]{1,0:T(8,128)} %pick_joining.1), channel_id=1, source_target_pairs={{16,0},{17,1},{18,2},{19,3},{20,4},{21,5},{22,6},{23,7},{24,8},{25... | collective-permute-start | bytes 2457608 | tf_op jit(solution)/shard_map/ppermute | solution.py:1057
  92.7 17.6 %collective-permute-start.14 = (f32[130,512]{1,0:T(8,128)}, f32[130,512]{1,0:T(8,128)}, u32[]{:S(2)}, u32[]{:S(2)}) collective-permute-start(f32[130,512]{1,0:T(8,128)} %select_maximum_fusion.3.refs_0_), channel_id=1, source_target_pairs={{0,16},{16,0},{1,17},{17,1},{2,18},{18,2},{3,19},{19,3},{4,20},{20... | collective-permute-start | bytes 798728 | tf_op jit(solution)/shard_map/ppermute | solution.py:1015
  93.9 110.4 %collective-permute-start.16 = (f32[3,400,512]{2,1,0:T(8,128)}, f32[3,400,512]{2,1,0:T(8,128)}, u32[]{:S(2)}, u32[]{:S(2)}) collective-permute-start(f32[3,400,512]{2,1,0:T(8,128)} %bitcast.82), channel_id=1, source_target_pairs={{0,16},{16,0},{1,17},{17,1},{2,18},{18,2},{3,19},{19,3},{4,20},{20... | collective-permute-start | bytes 7372808 | tf_op jit(solution)/shard_map/ppermute | solution.py:1015
  102.8 13.4 %all-to-all-start.15 = ((f32[16,2,2,512]{3,2,1,0:T(2,128)}), f32[16,2,2,512]{3,2,1,0:T(2,128)}, u32[]{:S(2)}, u32[]{:S(2)}) async-start(f32[16,2,2,512]{3,2,1,0:T(2,128)} %get-tuple-element.408), calls=%async_computation.15 | async-start | bytes 262144 | tf_op jit(solution)/shard_map/all_to_all | solution.py:42
  123.2 15.0 %all-to-all-start.16 = ((f32[16,2,2,640]{3,2,1,0:T(2,128)}), f32[16,2,2,640]{3,2,1,0:T(2,128)}, u32[]{:S(2)}, u32[]{:S(2)}) async-start(f32[16,2,2,640]{3,2,1,0:T(2,128)} %get-tuple-element.416), calls=%async_computation.16 | async-start | bytes 327680 | tf_op jit(solution)/shard_map/all_to_all | solution.py:42
  131.0 143.9 %copy-start.48 = (s32[6]{0:T(128)}, s32[6]{0:T(128)S(1)}, u32[]{:S(2)}) copy-start(s32[6]{0:T(128)S(1)} %pad_add_fusion.2.meta) | copy-start | bytes 76
  131.8 143.1 %copy-start.20 = (f32[6,512]{1,0:T(8,128)}, f32[6,512]{1,0:T(8,128)S(1)}, u32[]{:S(2)}) copy-start(f32[6,512]{1,0:T(8,128)S(1)} %get-tuple-element.543.refs_2_.refs_3_.refs_5_.refs_6_) | copy-start | bytes 36868
  131.8 143.1 %copy-start.22 = (f32[6,512]{1,0:T(8,128)}, f32[6,512]{1,0:T(8,128)S(1)}, u32[]{:S(2)}) copy-start(f32[6,512]{1,0:T(8,128)S(1)} %get-tuple-element.542.refs_3_.refs_4_.refs_6_.refs_7_) | copy-start | bytes 36868
  144.0 123.2 %copy-start.29 = (f32[2,2,512]{2,1,0:T(2,128)}, f32[2,2,512]{2,1,0:T(2,128)S(1)}, u32[]{:S(2)}) copy-start(f32[2,2,512]{2,1,0:T(2,128)S(1)} %get-tuple-element.419.refs_2_.refs_4_.refs_1_) | copy-start | bytes 24580
  144.1 14.5 %all-to-all-start.17 = ((f32[16,2,2,512]{3,2,1,0:T(2,128)}), f32[16,2,2,512]{3,2,1,0:T(2,128)}, u32[]{:S(2)}, u32[]{:S(2)}) async-start(f32[16,2,2,512]{3,2,1,0:T(2,128)} %get-tuple-element.418), calls=%async_computation.17 | async-start | bytes 262144 | tf_op jit(solution)/shard_map/all_to_all | solution.py:42
  164.4 12.0 %all-to-all-start.18 = ((f32[16,2,2,512]{3,2,1,0:T(2,128)}), f32[16,2,2,512]{3,2,1,0:T(2,128)}, u32[]{:S(2)}, u32[]{:S(2)}) async-start(f32[16,2,2,512]{3,2,1,0:T(2,128)} %get-tuple-element.421), calls=%async_computation.18 | async-start | bytes 262144 | tf_op jit(solution)/shard_map/all_to_all | solution.py:42
  200.7 11.3 %all-to-all-start.20 = ((f32[16,2,2,512]{3,2,1,0:T(2,128)}), f32[16,2,2,512]{3,2,1,0:T(2,128)S(1)}, u32[]{:S(2)}, u32[]{:S(2)}) async-start(f32[16,2,2,512]{3,2,1,0:T(2,128)} %get-tuple-element.427), calls=%async_computation.20 | async-start | bytes 262144 | tf_op jit(solution)/shard_map/all_to_all | solution.py:42
  242.0 11.5 %all-to-all-start.22 = ((f32[16,2,2,512]{3,2,1,0:T(2,128)}), f32[16,2,2,512]{3,2,1,0:T(2,128)S(1)}, u32[]{:S(2)}, u32[]{:S(2)}) async-start(f32[16,2,2,512]{3,2,1,0:T(2,128)} %get-tuple-element.439), calls=%async_computation.22 | async-start | bytes 262144 | tf_op jit(solution)/shard_map/all_to_all | solution.py:42
  261.9 19.1 %all-to-all-start.23 = ((f32[16,2,2,512]{3,2,1,0:T(2,128)}), f32[16,2,2,512]{3,2,1,0:T(2,128)S(1)}, u32[]{:S(2)}, u32[]{:S(2)}) async-start(f32[16,2,2,512]{3,2,1,0:T(2,128)} %get-tuple-element.445), calls=%async_computation.23 | async-start | bytes 262144 | tf_op jit(solution)/shard_map/all_to_all | solution.py:42
  267.2 148.9 %all-reduce.6.cloned.1.call-start = ((), (), s32[]{:S(2)}) async-start(), calls=%async_computation.24 | async-start | bytes 3145728 | tf_op jit(solution)/shard_map/psum | solution.py:1114
  280.9 8.9 %collective-permute-start.17 = (f32[768,512]{1,0:T(8,128)}, f32[768,512]{1,0:T(8,128)}, u32[]{:S(2)}, u32[]{:S(2)}) collective-permute-start(f32[768,512]{1,0:T(8,128)} %get-tuple-element.462), channel_id=1, source_target_pairs={{0,16},{16,0},{1,17},{17,1},{2,18},{18,2},{3,19},{19,3},{4,20},{20... | collective-permute-start | bytes 4718600 | tf_op jit(solution)/shard_map/ppermute | solution.py:1015
  292.8 313.1 %all-reduce.8.cloned.1.call-start = ((), (), s32[]{:S(2)}) async-start(), calls=%async_computation.25 | async-start | bytes 6815744 | tf_op jit(solution)/shard_map/psum | solution.py:1137
  293.6 17.6 %all-to-all-start = ((f32[16,2,2,512]{3,2,1,0:T(2,128)}), f32[16,2,2,512]{3,2,1,0:T(2,128)S(1)}, u32[]{:S(2)}, u32[]{:S(2)}) async-start(f32[16,2,2,512]{3,2,1,0:T(2,128)} %get-tuple-element.157), calls=%async_computation | async-start | bytes 262144 | tf_op jit(solution)/shard_map/cond/branch_1_fun/all_to_all | solution.py:42
  320.0 12.3 %all-to-all-start.1 = ((f32[16,2,2,512]{3,2,1,0:T(2,128)}), f32[16,2,2,512]{3,2,1,0:T(2,128)S(1)}, u32[]{:S(2)}, u32[]{:S(2)}) async-start(f32[16,2,2,512]{3,2,1,0:T(2,128)} %get-tuple-element.171), calls=%async_computation.1 | async-start | bytes 262144 | tf_op jit(solution)/shard_map/cond/branch_1_fun/all_to_all | solution.py:42
  342.5 13.9 %all-to-all-start.2 = ((f32[16,2,4,512]{3,2,1,0:T(4,128)}), f32[16,2,4,512]{3,2,1,0:T(4,128)}, u32[]{:S(2)}, u32[]{:S(2)}) async-start(f32[16,2,4,512]{3,2,1,0:T(4,128)} %get-tuple-element.204), calls=%async_computation.2 | async-start | bytes 524288 | tf_op jit(solution)/shard_map/cond/branch_1_fun/all_to_all | solution.py:42
  363.6 12.2 %all-to-all-start.3 = ((f32[16,2,2,512]{3,2,1,0:T(2,128)}), f32[16,2,2,512]{3,2,1,0:T(2,128)}, u32[]{:S(2)}, u32[]{:S(2)}) async-start(f32[16,2,2,512]{3,2,1,0:T(2,128)} %get-tuple-element.211), calls=%async_computation.3 | async-start | bytes 262144 | tf_op jit(solution)/shard_map/cond/branch_1_fun/all_to_all | solution.py:42
  375.8 36.0 %collective-permute-start = (f32[896,512]{1,0:T(8,128)}, f32[896,512]{1,0:T(8,128)}, u32[]{:S(2)}, u32[]{:S(2)}) collective-permute-start(f32[896,512]{1,0:T(8,128)} %get-tuple-element.220), channel_id=1, source_target_pairs={{0,16},{16,0},{1,17},{17,1},{2,18},{18,2},{3,19},{19,3},{4,20},{20... | collective-permute-start | bytes 5505032 | tf_op jit(solution)/shard_map/cond/branch_1_fun/ppermute | solution.py:1015
  383.5 17.8 %all-to-all-start.4 = ((f32[16,2,2,512]{3,2,1,0:T(2,128)}), f32[16,2,2,512]{3,2,1,0:T(2,128)}, u32[]{:S(2)}, u32[]{:S(2)}) async-start(f32[16,2,2,512]{3,2,1,0:T(2,128)} %get-tuple-element.229), calls=%async_computation.4 | async-start | bytes 262144 | tf_op jit(solution)/shard_map/cond/branch_1_fun/all_to_all | solution.py:42
  401.3 8.5 %collective-permute-start.1 = (f32[768,512]{1,0:T(8,128)}, f32[768,512]{1,0:T(8,128)}, u32[]{:S(2)}, u32[]{:S(2)}) collective-permute-start(f32[768,512]{1,0:T(8,128)} %get-tuple-element.236), channel_id=1, source_target_pairs={{0,16},{16,0},{1,17},{17,1},{2,18},{18,2},{3,19},{19,3},{4,20},{20... | collective-permute-start | bytes 4718600 | tf_op jit(solution)/shard_map/cond/branch_1_fun/ppermute | solution.py:1015
  416.9 14.8 %all-to-all-start.5 = ((f32[16,2,2,512]{3,2,1,0:T(2,128)}), f32[16,2,2,512]{3,2,1,0:T(2,128)S(1)}, u32[]{:S(2)}, u32[]{:S(2)}) async-start(f32[16,2,2,512]{3,2,1,0:T(2,128)} %get-tuple-element.247), calls=%async_computation.5 | async-start | bytes 262144 | tf_op jit(solution)/shard_map/cond/branch_1_fun/all_to_all | solution.py:42
  440.4 15.4 %all-to-all-start.6 = ((f32[16,2,2,512]{3,2,1,0:T(2,128)}), f32[16,2,2,512]{3,2,1,0:T(2,128)S(1)}, u32[]{:S(2)}, u32[]{:S(2)}) async-start(f32[16,2,2,512]{3,2,1,0:T(2,128)} %get-tuple-element.261), calls=%async_computation.6 | async-start | bytes 262144 | tf_op jit(solution)/shard_map/cond/branch_1_fun/all_to_all | solution.py:42
  470.3 4.0 collective-permute-start.2
  477.4 33.9 %collective-permute-start.4 = (f32[2,400,512]{2,1,0:T(8,128)}, f32[2,400,512]{2,1,0:T(8,128)}, u32[]{:S(2)}, u32[]{:S(2)}) collective-permute-start(f32[2,400,512]{2,1,0:T(8,128)} %get-tuple-element.279), channel_id=1, source_target_pairs={{0,16},{1,17},{2,18},{3,19},{4,20},{5,21},{6,22},{7,23},{8,24},{9,... | collective-permute-start | bytes 4915208 | tf_op jit(solution)/shard_map/cond/branch_1_fun/ppermute | solution.py:1056
  480.7 34.2 %collective-permute-start.7 = (f32[768,512]{1,0:T(8,128)}, f32[768,512]{1,0:T(8,128)}, u32[]{:S(2)}, u32[]{:S(2)}) collective-permute-start(f32[768,512]{1,0:T(8,128)} %get-tuple-element.286), channel_id=1, source_target_pairs={{0,16},{1,17},{2,18},{3,19},{4,20},{5,21},{6,22},{7,23},{8,24},{9,... | collective-permute-start | bytes 4718600 | tf_op jit(solution)/shard_map/cond/branch_1_fun/ppermute | solution.py:1056
  483.1 26.5 %all-to-all-start.7 = ((f32[4,224,512]{2,1,0:T(8,128)}), f32[4,224,512]{2,1,0:T(8,128)}, u32[]{:S(2)}, u32[]{:S(2)}) async-start(f32[4,224,512]{2,1,0:T(8,128)} %bitcast.86), calls=%async_computation.7 | async-start | bytes 3670016 | tf_op jit(solution)/shard_map/cond/branch_1_fun/all_to_all | solution.py:47
  487.6 18.1 %collective-permute-start.6 = (f32[2,200,512]{2,1,0:T(8,128)}, f32[2,200,512]{2,1,0:T(8,128)}, u32[]{:S(2)}, u32[]{:S(2)}) collective-permute-start(f32[2,200,512]{2,1,0:T(8,128)} %get-tuple-element.281), channel_id=1, source_target_pairs={{0,16},{1,17},{2,18},{3,19},{4,20},{5,21},{6,22},{7,23},{8,24},{9,... | collective-permute-start | bytes 2457608 | tf_op jit(solution)/shard_map/cond/branch_1_fun/ppermute | solution.py:1056
  491.9 15.2 %collective-permute-start.5 = (f32[1,400,512]{2,1,0:T(8,128)}, f32[1,400,512]{2,1,0:T(8,128)S(1)}, u32[]{:S(2)}, u32[]{:S(2)}) collective-permute-start(f32[1,400,512]{2,1,0:T(8,128)} %slice.129), channel_id=1, source_target_pairs={{16,0},{17,1},{18,2},{19,3},{20,4},{21,5},{22,6},{23,7},{24,8},{25... | collective-permute-start | bytes 2457608 | tf_op jit(solution)/shard_map/cond/branch_1_fun/ppermute | solution.py:1057
  495.3 16.0 %collective-permute-start.3 = (f32[1,200,512]{2,1,0:T(8,128)}, f32[1,200,512]{2,1,0:T(8,128)}, u32[]{:S(2)}, u32[]{:S(2)}) collective-permute-start(f32[1,200,512]{2,1,0:T(8,128)} %slice.127), channel_id=1, source_target_pairs={{16,0},{17,1},{18,2},{19,3},{20,4},{21,5},{22,6},{23,7},{24,8},{25... | collective-permute-start | bytes 1228808 | tf_op jit(solution)/shard_map/cond/branch_1_fun/ppermute | solution.py:1057
  557.8 33.6 %all-to-all-start.10 = ((f32[4,224,512]{2,1,0:T(8,128)}), f32[4,224,512]{2,1,0:T(8,128)}, u32[]{:S(2)}, u32[]{:S(2)}) async-start(f32[4,224,512]{2,1,0:T(8,128)} %broadcast_in_dim.20), calls=%async_computation.10 | async-start | bytes 3670016 | tf_op jit(solution)/shard_map/cond/branch_1_fun/all_to_all | solution.py:47
  605.9 8.9 %collective-permute-start.19 = (f32[1664,512]{1,0:T(8,128)}, f32[1664,512]{1,0:T(8,128)S(1)}, u32[]{:S(2)}, u32[]{:S(2)}) collective-permute-start(f32[1664,512]{1,0:T(8,128)} %all-reduce.8.cloned.1.call-done), channel_id=1, source_target_pairs={{0,16},{16,0},{1,17},{17,1},{2,18},{18,2},{3,19},{19,3},{4,20},{20... | collective-permute-start | bytes 10223624 | tf_op jit(solution)/shard_map/ppermute | solution.py:1015
  605.9 8.9 %collective-permute-start.18 = (f32[896,512]{1,0:T(8,128)}, f32[896,512]{1,0:T(8,128)S(1)}, u32[]{:S(2)}, u32[]{:S(2)}) collective-permute-start(f32[896,512]{1,0:T(8,128)} %get-tuple-element.488), channel_id=1, source_target_pairs={{16,0},{17,1},{18,2},{19,3},{20,4},{21,5},{22,6},{23,7},{24,8},{25... | collective-permute-start | bytes 5505032 | tf_op jit(solution)/shard_map/ppermute | solution.py:1057
  (62 other events, 691.9 us)
Sparse Core Ops, SparseCore 0:
  293.0 122.7 all-reduce.5
  423.0 182.8 all-reduce.7
where the time goes:
time: 645 us; the launch traced here: 632 us
  Pallas kernels  256 us (40%)
  starting transfers between devices  121 us (19%)
  waiting for transfers between devices  93 us (14%)
  blocking collectives  66.7 us (10%)
  other arithmetic  40.4 us (6%)
  local copies, waits for them, and re-layouts  31.5 us (5%)
  between operations  16 us (2%)
  loops' own time  6.75 us (1%)
    pallas_call x42, Pallas kernels, call(): pl.pallas_call(inner, out_shape=shapes, grid_spec=pltpu.PrefetchScalarGri...  256 us
    all_to_all x18, starting transfers between devices, exchange(): return lax.all_to_all(block, 'dp', 0, 0)  93.1 us
    all_to_all x18, waiting for transfers between devices, exchange(): return lax.all_to_all(block, 'dp', 0, 0)  47.6 us
    all_to_all x2, blocking collectives, exchange(): return lax.all_to_all(block, 'dp', 0, 0, axis_index_groups=groups)  41.3 us
    all_to_all x2, waiting for transfers between devices, exchange(): return lax.all_to_all(block, 'dp', 0, 0, axis_index_groups=groups)  26.2 us
    all_to_all x2, blocking collectives, exchange(): return lax.all_to_all(block, 'dp', 0, 0)  25.4 us
  transfers between devices with their start and end apart: 42, of which 21 were waited for; matrix products, arithmetic and copies ran while one was open for 8% of the time, Pallas kernels for 35%

commit v1 on v0

--- a/solution.py
+++ b/solution.py
@@ -1077,7 +1077,10 @@
     both = jnp.concatenate([length, half_len, flag, half_len, join_len, flag, picks[MB - 1 :]])
 
     def small(block):
-        t = jnp.where(first == (block == 0), taps, far_taps)
+        own, far = taps, far_taps
+        if block:
+            own, far, _ = lax.optimization_barrier((taps, far_taps, c14.z[3]))
+        t = jnp.where(first == (block == 0), own, far)
         return t[: 5 * TAPS].reshape(5, TAPS, C), t[5 * TAPS : 5 * TAPS + 6], t[5 * TAPS + 6 :]
 
     excitations = split_squeeze(meta1, squeeze, far_squeeze)
@@ -1093,7 +1096,7 @@
     c14 = Block(False, meta1, small(0), {**parts0[0][1], **parts0[1][1]}, stages)
     c14.x, c14.x_far, c14.first_matrix = inputs, far_rows, (pw[0], far_w0)
     c14.excitation = excitations[0]
-    c14.forward({2: (parts0[1][0],)})
+    c14.forward({1: excitations[0], 2: (parts0[1][0],)})
     late_picks, _ = lax.optimization_barrier((picks, c14.z[3]))
     far_joining = to_lower(pick_joining(late_picks, features.reshape(MB, 2, HALF, C)))
     c15 = Block(True, meta2, small(1), {**parts1[0][1], **parts1[1][1], **parts1[2][1]}, stages)
@@ -1162,23 +1165,21 @@
     came3 = to_lower(sum3)
     sum12, _ = lax.optimization_barrier((sum12, sum3))
     came12 = swap(sum12)
-    split = PIECE_ROWS[1]
-    sum1, sum2, came1, came2 = sum12[:split], sum12[split:], came12[:split], came12[split:]
-
-    lead = 3 * C // 2
-
-    def joined(near, far):
-        pair = [x.reshape(-1, 1, C // 2, C) for x in (near, far)]
-        both = jnp.where(first, jnp.concatenate(pair, axis=1), jnp.concatenate(pair[::-1], axis=1))
-        return both.reshape(-1, C, C)
-
-    choose_mine = lambda a, b: jnp.where(first, a, b)
-    rest_part = joined(choose_mine(sum3[:lead], sum1[:lead]), choose_mine(came3[:lead], came1[:lead]))
-    lead_part = joined(choose_mine(sum2[:C], sum0[:C]), choose_mine(came2[:C], came0[:C]))
-    pw_grad = jnp.concatenate([rest_part, lead_part], axis=0)[None]
-    res_grad = joined(choose_mine(sum2[C:], sum0[C:]), choose_mine(came2[C:], came0[C:]))
-    near, far = choose_mine(sum3[lead:], sum1[lead:]), choose_mine(came3[lead:], came1[lead:])
-    rows = jnp.where(first, jnp.concatenate([near, far], axis=0), jnp.concatenate([far, near], axis=0))
+    split, lead = PIECE_ROWS[1], 3 * C // 2
+
+    def assembled(rest_top, rest_bottom, lead_top, lead_bottom):
+        halves_of = lambda x: x.reshape(-1, 1, C // 2, C)
+        both = lambda top, bottom: jnp.concatenate([halves_of(top), halves_of(bottom)], axis=1).reshape(-1, C, C)
+        rest, top = both(rest_top[:lead], rest_bottom[:lead]), both(lead_top[:C], lead_bottom[:C])
+        res = both(lead_top[C:], lead_bottom[C:])
+        return jnp.concatenate([rest, top], axis=0)[None], res, jnp.concatenate([rest_top[lead:], rest_bottom[lead:]], axis=0)
+
+    pw_grad, res_grad, rows = lax.cond(
+        first,
+        lambda s3, c3, s12, c12, s0, c0: assembled(s3, c3, s12[split:], c12[split:]),
+        lambda s3, c3, s12, c12, s0, c0: assembled(c12[:split], s12[:split], c0, s0),
+        sum3, came3, sum12, came12, sum0, came0,
+    )
     dw_grad = rows[TAIL_ROWS : TAIL_ROWS + 40].reshape(1, 5, 8, C)
     norms = jnp.concatenate([dw_grad[0, 1:, TAPS : TAPS + 2], rows[None, 2 * SE + 2 : 2 * SE + 4], rows[None, 2 * SE + 4 : 2 * SE + 6]], axis=0)
     return (

time: 645 us -> 644 us (level)
  blocking collectives: 66.7 us -> 100 us
  waiting for transfers between devices: 93 us -> 69.7 us
  other arithmetic: 40.4 us -> 31.6 us
    all_to_all x2 -> x3, blocking collectives: 41.3 us -> 75.1 us  [exchange(): return lax.all_to_all(block, 'dp', 0, 0, axis_index_groups=groups)]
    all_to_all x2 -> x1, waiting for transfers between devices: 26.2 us -> 0.01 us  [exchange(): return lax.all_to_all(block, 'dp', 0, 0, axis_index_groups=groups)]
    select_n x11 -> x2, other arithmetic: 8.63 us -> 0.75 us  [small(): t = jnp.where(first == (block == 0), own, far)]
  transfers between devices with their start and end apart: 42 -> 41, of which waited for: 21 -> 20; matrix products, arithmetic and copies ran while one was open for 8% -> 7% of each run, Pallas kernels for 35% -> 35%
where the time goes in v1:
time: 644 us; the launch traced here: 631 us
  Pallas kernels  255 us (40%)
  starting transfers between devices  117 us (18%)
  blocking collectives  100 us (16%)
  waiting for transfers between devices  69.7 us (11%)
  local copies, waits for them, and re-layouts  34.8 us (5%)
  other arithmetic  31.6 us (5%)
  between operations  15.1 us (2%)
  loops' own time  6.71 us (1%)
    pallas_call x42, Pallas kernels, call(): pl.pallas_call(inner, out_shape=shapes, grid_spec=pltpu.PrefetchScalarGri...  255 us
    all_to_all x18, starting transfers between devices, exchange(): return lax.all_to_all(block, 'dp', 0, 0)  96.2 us
    all_to_all x3, blocking collectives, exchange(): return lax.all_to_all(block, 'dp', 0, 0, axis_index_groups=groups)  75.1 us
    all_to_all x18, waiting for transfers between devices, exchange(): return lax.all_to_all(block, 'dp', 0, 0)  44.2 us
    all_to_all x2, blocking collectives, exchange(): return lax.all_to_all(block, 'dp', 0, 0)  25.4 us
  transfers between devices with their start and end apart: 41, of which 20 were waited for; matrix products, arithmetic and copies ran while one was open for 7% of the time, Pallas kernels for 35%

profile of v1, /device:TPU:0, one launch (start us, length us, event | category | flops | bytes accessed | tf_op | source)
XLA Modules:
  0.0 631.3 jit_solution(15548763497422054838)
XLA Ops:
  26.4 7.9 %all-to-all-start.11 = ((f32[16,2,2,640]{3,2,1,0:T(2,128)}), f32[16,2,2,640]{3,2,1,0:T(2,128)}, u32[]{:S(2)}, u32[]{:S(2)}) async-start(f32[16,2,2,640]{3,2,1,0:T(2,128)} %get-tuple-element.424), calls=%async_computation.11 | async-start | bytes 327680 | tf_op jit(solution)/shard_map/all_to_all | solution.py:42
  44.1 5.9 c14_forward_1.1
  49.9 6.9 %all-to-all-start.12 = ((f32[16,2,2,512]{3,2,1,0:T(2,128)}), f32[16,2,2,512]{3,2,1,0:T(2,128)}, u32[]{:S(2)}, u32[]{:S(2)}) async-start(f32[16,2,2,512]{3,2,1,0:T(2,128)} %get-tuple-element.430), calls=%async_computation.12 | async-start | bytes 262144 | tf_op jit(solution)/shard_map/all_to_all | solution.py:42
  64.7 5.9 c14_forward_2.1
  82.9 5.9 c14_forward_3.1
  118.7 7.0 %c14_tail_c15_forward_0.1 = (f32[2,400,512]{2,1,0:T(8,128)}, f32[2,2,512]{2,1,0:T(2,128)}, f32[2,2,512]{2,1,0:T(2,128)}, f32[2,8,512]{2,1,0:T(8,128)}, f32[2,64,...) custom-call(s32[11]{0:T(128)S(1)} %concatenate.78.meta, ...), custom_call_target="tpu_custom_call" | custom-call | flops 1258291200 | bytes 10297600 | tf_op jit(solution)/shard_map/c14_tail_c15_forward_0/pallas_call | solution.py:211
  125.6 6.2 all-to-all-start.16
  132.5 6.0 prepare_1_1.1.refs_5_.refs_6_.refs_7_.refs_2_
  139.8 5.8 c15_forward_1.1
  145.6 6.6 %all-to-all-start.17 = ((f32[16,2,2,512]{3,2,1,0:T(2,128)}), f32[16,2,2,512]{3,2,1,0:T(2,128)}, u32[]{:S(2)}, u32[]{:S(2)}) async-start(f32[16,2,2,512]{3,2,1,0:T(2,128)} %get-tuple-element.446), calls=%async_computation.17 | async-start | bytes 262144 | tf_op jit(solution)/shard_map/all_to_all | solution.py:42
  160.1 5.8 c15_forward_2.1
  177.9 5.9 c15_forward_3.1
  183.7 12.7 %all_to_all.112.refs_1_.refs_3_ = f32[16,2,4,512]{3,2,1,0:T(4,128)} all-to-all(f32[16,2,4,512]{3,2,1,0:T(4,128)} %get-tuple-element.453), channel_id=1, replica_groups=mesh['section'=2,'dp'=16] {'dp'}, dimensions={0} | all-to-all | bytes 524288 | tf_op jit(solution)/shard_map/all_to_all | solution.py:42
  196.4 5.9 c15_forward_4.1
  205.9 7.8 %all-to-all-done.20.refs_1_ = f32[16,2,2,512]{3,2,1,0:T(2,128)S(1)} async-done(((f32[16,2,2,512]{3,2,1,0:T(2,128)}), f32[16,2,2,512]{3,2,1,0:T(2,128)S(1)}, u32[]{:S(2)}, u32[]{:S(2)}) %all-to-all-start.20) | async-done | bytes 131104 | tf_op jit(solution)/shard_map/all_to_all | solution.py:42
  214.3 8.9 %c15_tail.1 = (f32[2,400,512]{2,1,0:T(8,128)}, f32[2,2,512]{2,1,0:T(2,128)}, f32[2,2,512]{2,1,0:T(2,128)}, f32[2,8,512]{2,1,0:T(8,128)}, f32[2,64,8]{2,1,0:T(8,1...) custom-call(s32[6]{0:T(128)} %copy-done.48, ...), custom_call_target="tpu_custom_call" | custom-call | bytes 14670080 | tf_op jit(solution)/shard_map/c15_tail/pallas_call | solution.py:211
  223.2 12.7 %all_to_all.113.refs_3_.refs_0_ = f32[16,2,4,512]{3,2,1,0:T(4,128)} all-to-all(f32[16,2,4,512]{3,2,1,0:T(4,128)} %get-tuple-element.462), channel_id=1, replica_groups=mesh['section'=2,'dp'=16] {'dp'}, dimensions={0} | all-to-all | bytes 524288 | tf_op jit(solution)/shard_map/all_to_all | solution.py:42
  235.9 8.1 %c15_backward_4.1 = (f32[256,512]{1,0:T(8,128)S(1)}, bf16[2,400,1024]{2,1,0:T(8,128)(2,1)}, f32[2,400,512]{2,1,0:T(8,128)}, f32[16,2,2,512]{3,2,1,0:T(2,128)}) custom-call(s32[6]{0:T(128)S(1)} %copy-done.49, f32[2,400,512]{2,1,0:T(8,128)} %get-tuple-element.461.refs_0_, ...), custom_call_target="tpu_custom_call", output_to_operand_aliasing={{0}: (12, {})} | custom-call | flops 1258291200 | bytes 11307008 | tf_op jit(solution)/shard_map/c15_backward_4/pallas_call | solution.py:211
  247.8 6.1 c15_weights_4.1
  256.2 7.9 %c15_backward_3.1 = (f32[256,512]{1,0:T(8,128)S(1)}, bf16[2,400,1024]{2,1,0:T(8,128)(2,1)}, f32[2,400,512]{2,1,0:T(8,128)}, f32[16,2,2,512]{3,2,1,0:T(2,128)}) custom-call(s32[6]{0:T(128)S(1)} %copy-done.49, f32[2,400,512]{2,1,0:T(8,128)} %get-tuple-element.466.refs_0_, ...), custom_call_target="tpu_custom_call", output_to_operand_aliasing={{0}: (13, {})} | custom-call | flops 1258291200 | bytes 12224512 | tf_op jit(solution)/shard_map/c15_backward_3/pallas_call | solution.py:211
  269.4 7.6 %c15_residual_back.1 = (f32[768,512]{1,0:T(8,128)}, f32[768,512]{1,0:T(8,128)}, f32[2,400,512]{2,1,0:T(8,128)}) custom-call(s32[6]{0:T(128)S(1)} %copy-done.49, f32[16,2,4,512]{3,2,1,0:T(4,128)} %all_to_all.113.refs_3_.refs_0_, f32[2,2,512]{2,1,0:T(2,128)S(1)} %copy-done.25, ...), custom_call_target="tpu_custom_call", output_to_operand_aliasing={{0}: (9, {}), {1}: (10, {})} | custom-call | flops 2516582400 | bytes 12087296 | tf_op jit(solution)/shard_map/c15_residual_back/pallas_call | solution.py:211
  277.0 6.0 c15_weights_3.1
  283.7 7.9 %c15_backward_2.1 = (f32[256,512]{1,0:T(8,128)S(1)}, bf16[2,400,1024]{2,1,0:T(8,128)(2,1)}, f32[2,400,512]{2,1,0:T(8,128)}, f32[16,2,2,512]{3,2,1,0:T(2,128)}) custom-call(s32[6]{0:T(128)S(1)} %copy-done.49, f32[2,400,512]{2,1,0:T(8,128)} %get-tuple-element.472.refs_0_, ...), custom_call_target="tpu_custom_call", output_to_operand_aliasing={{0}: (13, {})} | custom-call | flops 1258291200 | bytes 12224512 | tf_op jit(solution)/shard_map/c15_backward_2/pallas_call | solution.py:211
  295.0 123.3 %conditional.3 = (f32[2,200,512]{2,1,0:T(8,128)}, f32[1664,512]{1,0:T(8,128)}, f32[2,400,512]{2,1,0:T(8,128)}, f32[2,208,512]{2,1,0:T(8,128)}, bf16[2,400,1024]{...) conditional(s32[]{:T(128)} %bitcast.42, () %tuple.53, (f32[16,2,2,512]{3,2,1,0:T(2,128)}, ...), branch_computations={%region_0.1_spmd, %region_1.2_spmd} | conditional | flops 12685410304 | bytes 164675456 | solution.py:1020
  295.1 7.3 %all-to-all-start = ((f32[16,2,2,512]{3,2,1,0:T(2,128)}), f32[16,2,2,512]{3,2,1,0:T(2,128)S(1)}, u32[]{:S(2)}, u32[]{:S(2)}) async-start(f32[16,2,2,512]{3,2,1,0:T(2,128)} %get-tuple-element.171), calls=%async_computation | async-start | bytes 262144 | tf_op jit(solution)/shard_map/cond/branch_1_fun/all_to_all | solution.py:42
  302.5 6.1 c15_weights_2.1
  313.4 8.2 %c15_backward_1.1 = (f32[256,512]{1,0:T(8,128)S(1)}, bf16[2,400,1024]{2,1,0:T(8,128)(2,1)}, f32[2,400,512]{2,1,0:T(8,128)}, f32[16,2,2,512]{3,2,1,0:T(2,128)}) custom-call(s32[6]{0:T(128)S(1)} %get-tuple-element.167.meta, f32[2,400,512]{2,1,0:T(8,128)} %get-tuple-element.168.refs_0_, ...), custom_call_target="tpu_custom_call", output_to_operand_aliasing={{0}: (14, {})} | custom-call | flops 1258291200 | bytes 12224512 | tf_op jit(solution)/shard_map/cond/branch_1_fun/c15_backward_1/pallas_call | solution.py:211
  326.4 6.0 c15_weights_1.1
  334.9 9.5 %c15_backward_0_c14_tail_back.1 = (f32[256,512]{1,0:T(8,128)S(1)}, bf16[2,400,1024]{2,1,0:T(8,128)(2,1)}, f32[2,200,512]{2,1,0:T(8,128)}, f32[2,200,512]{2,1,0:T...) custom-call(s32[11]{0:T(128)} %get-tuple-element.166.meta, ...), custom_call_target="tpu_custom_call", output_to_operand_aliasing={{0}: (30, {})} | custom-call | flops 1258291200 | bytes 24387840 | tf_op jit(solution)/shard_map/cond/branch_1_fun/c15_backward_0_c14_tail_back/pallas_call | solution.py:211
  349.6 5.8 c15_weights_0.1
  358.3 7.1 %c14_backward_4.1 = (f32[256,512]{1,0:T(8,128)S(1)}, bf16[2,208,1024]{2,1,0:T(8,128)(2,1)}, f32[2,400,512]{2,1,0:T(8,128)}, f32[16,2,2,512]{3,2,1,0:T(2,128)}) custom-call(s32[5]{0:T(128)S(1)} %copy-done.45, f32[2,208,512]{2,1,0:T(8,128)} %get-tuple-element.216.refs_0_, ...), custom_call_target="tpu_custom_call", output_to_operand_aliasing={{0}: (13, {})} | custom-call | flops 654311424 | bytes 9996288 | tf_op jit(solution)/shard_map/cond/branch_1_fun/c14_backward_4/pallas_call | solution.py:211
  377.6 7.8 %c14_backward_3.1 = (f32[256,512]{1,0:T(8,128)S(1)}, bf16[2,400,1024]{2,1,0:T(8,128)(2,1)}, f32[2,400,512]{2,1,0:T(8,128)}, f32[16,2,2,512]{3,2,1,0:T(2,128)}) custom-call(s32[5]{0:T(128)S(1)} %copy-done.45, f32[2,400,512]{2,1,0:T(8,128)} %get-tuple-element.224.refs_0_, ...), custom_call_target="tpu_custom_call", output_to_operand_aliasing={{0}: (13, {})} | custom-call | flops 1258291200 | bytes 12224512 | tf_op jit(solution)/shard_map/cond/branch_1_fun/c14_backward_3/pallas_call | solution.py:211
  391.0 5.9 c14_residual_back.1
  396.9 6.1 c14_weights_3.1
  403.7 7.8 %c14_backward_2.1 = (f32[256,512]{1,0:T(8,128)S(1)}, bf16[2,400,1024]{2,1,0:T(8,128)(2,1)}, f32[2,400,512]{2,1,0:T(8,128)}, f32[16,2,2,512]{3,2,1,0:T(2,128)}) custom-call(s32[5]{0:T(128)S(1)} %copy-done.45, f32[2,400,512]{2,1,0:T(8,128)} %get-tuple-element.231.refs_0_, ...), custom_call_target="tpu_custom_call", output_to_operand_aliasing={{0}: (13, {})} | custom-call | flops 1258291200 | bytes 11175936 | tf_op jit(solution)/shard_map/cond/branch_1_fun/c14_backward_2/pallas_call | solution.py:211
  419.2 173.6 %conditional.4 = (f32[768,512]{1,0:T(8,128)}, f32[896,512]{1,0:T(8,128)}, f32[1,1200,512]{2,1,0:T(8,128)}, f32[1,1200,512]{2,1,0:T(8,128)}) conditional(s32[]{:T(128)} %bitcast.42, () %tuple.52, (f32[16,2,2,512]{3,2,1,0:T(2,128)}, s32[5]{0:T(128)S(1)}, f32[2,400,512]{2,1,0:T(8,128)}, f32[2,2,512]{2,1,0:T(2,128)S(1)}, f32[6,512]{1,0:T(8,128)S(1)}, ...), branch_computations={%region_3.4_spmd, %region_4.10_spmd} | conditional | flops 6300770304 | bytes 135285952 | solution.py:1020
  419.2 6.9 %all-to-all-start.5 = ((f32[16,2,2,512]{3,2,1,0:T(2,128)}), f32[16,2,2,512]{3,2,1,0:T(2,128)S(1)}, u32[]{:S(2)}, u32[]{:S(2)}) async-start(f32[16,2,2,512]{3,2,1,0:T(2,128)} %get-tuple-element.261), calls=%async_computation.5 | async-start | bytes 262144 | tf_op jit(solution)/shard_map/cond/branch_1_fun/all_to_all | solution.py:42
  426.1 6.1 c14_weights_2.1
  434.6 8.0 %c14_backward_1.1 = (f32[256,512]{1,0:T(8,128)S(1)}, bf16[2,400,1024]{2,1,0:T(8,128)(2,1)}, f32[2,400,512]{2,1,0:T(8,128)}, f32[16,2,2,512]{3,2,1,0:T(2,128)}) custom-call(s32[5]{0:T(128)S(1)} %get-tuple-element.255.meta, f32[2,400,512]{2,1,0:T(8,128)} %get-tuple-element.258.refs_0_, ...), custom_call_target="tpu_custom_call", output_to_operand_aliasing={{0}: (14, {})} | custom-call | flops 1258291200 | bytes 11175936 | tf_op jit(solution)/shard_map/cond/branch_1_fun/c14_backward_1/pallas_call | solution.py:211
  447.8 6.1 c14_weights_1.1
  458.8 7.3 %c14_backward_0.1 = (f32[256,512]{1,0:T(8,128)S(1)}, bf16[2,400,1024]{2,1,0:T(8,128)(2,1)}, f32[2,400,512]{2,1,0:T(8,128)}) custom-call(s32[5]{0:T(128)S(1)} %get-tuple-element.255.meta, f32[2,400,512]{2,1,0:T(8,128)} %get-tuple-element.273.refs_0_, f32[2,400,512]{2,1,0:T(8,128)} %get-tuple-element.267.refs_9_.refs_0_.refs_1_, ...), custom_call_target="tpu_custom_call", output_to_operand_aliasing={{0}: (14, {})} | custom-call | flops 1258291200 | bytes 12478464 | tf_op jit(solution)/shard_map/cond/branch_1_fun/c14_backward_0/pallas_call | solution.py:211
  466.1 5.6 c14_weights_0.1
  517.2 18.6 %all_to_all.109 = f32[4,56,512]{2,1,0:T(8,128)S(1)} all-to-all(f32[4,56,512]{2,1,0:T(8,128)S(1)} %bitcast.129), channel_id=1, replica_groups={{0,4,8,12},{1,5,9,13},{2,6,10,14},{3,7,11,15},{16,20,24,28},{17,21,25,2..., dimensions={0} | all-to-all | bytes 917504 | tf_op jit(solution)/shard_map/cond/branch_1_fun/all_to_all | solution.py:47
  535.9 21.3 %all_to_all.110 = f32[4,56,512]{2,1,0:T(8,128)S(1)} all-to-all(f32[4,56,512]{2,1,0:T(8,128)S(1)} %broadcast_in_dim.12), channel_id=1, replica_groups={{0,4,8,12},{1,5,9,13},{2,6,10,14},{3,7,11,15},{16,20,24,28},{17,21,25,2..., dimensions={0} | all-to-all | bytes 917504 | tf_op jit(solution)/shard_map/cond/branch_1_fun/all_to_all | solution.py:47
  557.5 35.1 %all_to_all.111 = f32[4,224,512]{2,1,0:T(8,128)} all-to-all(f32[4,224,512]{2,1,0:T(8,128)S(1)} %broadcast_in_dim.20), channel_id=1, replica_groups={{0,1,2,3},{4,5,6,7},{8,9,10,11},{12,13,14,15},{16,17,18,19},{20,21,22,2..., dimensions={0} | all-to-all | bytes 3670016 | tf_op jit(solution)/shard_map/cond/branch_1_fun/all_to_all | solution.py:47
  592.8 11.4 %all-reduce.8.cloned.1.call-done = f32[1664,512]{1,0:T(8,128)} async-done(((f32[1664,512]{1,0:T(8,128)}), f32[1664,512]{1,0:T(8,128)}) %all-reduce.8.cloned.1.call-update) | async-done | bytes 3407888 | tf_op jit(solution)/shard_map/psum | solution.py:1140
  605.6 7.5 %collective-permute-done.19 = f32[896,512]{1,0:T(8,128)S(1)} collective-permute-done((f32[896,512]{1,0:T(8,128)}, f32[896,512]{1,0:T(8,128)S(1)}, u32[]{:S(2)}, u32[]{:S(2)}) %collective-permute-start.19) | collective-permute-done | bytes 1835040 | tf_op jit(solution)/shard_map/ppermute | solution.py:1057
  613.1 6.8 %conditional.5 = (f32[1,5,512,512]{3,2,1,0:T(8,128)S(1)}, f32[1,512,512]{2,1,0:T(8,128)S(1)}, f32[256,512]{1,0:T(8,128)S(1)}) conditional(s32[]{:T(128)} %convert_element_type.15, (f32[1664,512]{1,0:T(8,128)S(1)}, f32[1664,512]{1,0:T(8,128)}, f32[768,512]{1,0:T(8,128)}, f32[768,512]{1,0:T(8,128)}) %tuple.62, (f32[896,512]{1,0:T(8,128)}, ...), branch_computations={%region_11.12_spmd, %region_12.13_spmd} | conditional | flops 3014656 | bytes 51380276 | solution.py:1177
  (295 shorter events, 230.7 us)
Async XLA Ops:
  7.2 33.0 %collective-permute-start.12 = (f32[5,512,512]{2,1,0:T(8,128)}, f32[5,512,512]{2,1,0:T(8,128)}, u32[]{:S(2)}, u32[]{:S(2)}) collective-permute-start(f32[5,512,512]{2,1,0:T(8,128)} %bitcast.103), channel_id=1, source_target_pairs={{0,16},{16,0},{1,17},{17,1},{2,18},{18,2},{3,19},{19,3},{4,20},{20... | collective-permute-start | bytes 15728648 | tf_op jit(solution)/shard_map/ppermute | solution.py:1015
  7.7 8.4 %collective-permute-start.8 = (s32[3]{0:T(128)}, s32[3]{0:T(128)S(1)}, u32[]{:S(2)}, u32[]{:S(2)}) collective-permute-start(s32[3]{0:T(128)} %bitcast.136), channel_id=1, source_target_pairs={{0,16},{16,0},{1,17},{17,1},{2,18},{18,2},{3,19},{19,3},{4,20},{20... | collective-permute-start | bytes 44 | tf_op jit(solution)/shard_map/ppermute | solution.py:1015
  9.9 10.9 %collective-permute-start.9 = (f32[400,512]{1,0:T(8,128)}, f32[400,512]{1,0:T(8,128)S(1)}, u32[]{:S(2)}, u32[]{:S(2)}) collective-permute-start(f32[400,512]{1,0:T(8,128)} %slice_bitcast_fusion.5), channel_id=1, source_target_pairs={{0,16},{1,17},{2,18},{3,19},{4,20},{5,21},{6,22},{7,23},{8,24},{9,... | collective-permute-start | bytes 2457608 | tf_op jit(solution)/shard_map/ppermute | solution.py:1056
  14.7 6.1 collective-permute-start.11
  15.5 3.0 collective-permute-start.10
  16.1 40.7 %collective-permute-start.14 = (f32[512,512]{1,0:T(8,128)}, f32[512,512]{1,0:T(8,128)}, u32[]{:S(2)}, u32[]{:S(2)}) collective-permute-start(f32[512,512]{1,0:T(8,128)} %bitcast.122), channel_id=1, source_target_pairs={{0,16},{16,0},{1,17},{17,1},{2,18},{18,2},{3,19},{19,3},{4,20},{20... | collective-permute-start | bytes 3145736 | tf_op jit(solution)/shard_map/ppermute | solution.py:1015
  17.6 114.9 %copy-start.41 = (s32[5]{0:T(128)}, s32[5]{0:T(128)S(1)}, u32[]{:S(2)}) copy-start(s32[5]{0:T(128)S(1)} %pad_add_fusion.3.meta) | copy-start | bytes 64
  20.8 274.2 %copy-start.5 = (f32[5,5,512]{2,1,0:T(8,128)}, f32[5,5,512]{2,1,0:T(8,128)S(1)}, u32[]{:S(2)}) copy-start(f32[5,5,512]{2,1,0:T(8,128)S(1)} %reshape.157.refs_2_.refs_4_.refs_5_.refs_6_) | copy-start | bytes 153604
  26.4 17.6 %all-to-all-start.11 = ((f32[16,2,2,640]{3,2,1,0:T(2,128)}), f32[16,2,2,640]{3,2,1,0:T(2,128)}, u32[]{:S(2)}, u32[]{:S(2)}) async-start(f32[16,2,2,640]{3,2,1,0:T(2,128)} %get-tuple-element.424), calls=%async_computation.11 | async-start | bytes 327680 | tf_op jit(solution)/shard_map/all_to_all | solution.py:42
  35.4 1.6 collective-permute-start.13
  40.2 78.5 %copy-start.47 = (f32[64,1]{1,0:T(8,128)}, f32[64,1]{1,0:T(8,128)S(1)}, u32[]{:S(2)}) copy-start(f32[64,1]{1,0:T(8,128)S(1)} %get-tuple-element.426.refs_7_.refs_8_) | copy-start | bytes 772
  40.2 78.5 %copy-start.63 = (f32[1,512]{1,0:T(1,128)}, f32[1,512]{1,0:T(1,128)S(1)}, u32[]{:S(2)}) copy-start(f32[1,512]{1,0:T(1,128)S(1)} %get-tuple-element.428.refs_9_.refs_10_) | copy-start | bytes 6148
  49.9 68.7 %copy-start.21 = (f32[2,2,512]{2,1,0:T(2,128)}, f32[2,2,512]{2,1,0:T(2,128)S(1)}, u32[]{:S(2)}) copy-start(f32[2,2,512]{2,1,0:T(2,128)S(1)} %get-tuple-element.431.refs_2_.refs_4_) | copy-start | bytes 24580
  49.9 14.8 %all-to-all-start.12 = ((f32[16,2,2,512]{3,2,1,0:T(2,128)}), f32[16,2,2,512]{3,2,1,0:T(2,128)}, u32[]{:S(2)}, u32[]{:S(2)}) async-start(f32[16,2,2,512]{3,2,1,0:T(2,128)} %get-tuple-element.430), calls=%async_computation.12 | async-start | bytes 262144 | tf_op jit(solution)/shard_map/all_to_all | solution.py:42
  70.6 12.3 %all-to-all-start.13 = ((f32[16,2,2,512]{3,2,1,0:T(2,128)}), f32[16,2,2,512]{3,2,1,0:T(2,128)}, u32[]{:S(2)}, u32[]{:S(2)}) async-start(f32[16,2,2,512]{3,2,1,0:T(2,128)} %get-tuple-element.433), calls=%async_computation.13 | async-start | bytes 262144 | tf_op jit(solution)/shard_map/all_to_all | solution.py:42
  88.8 12.7 %all-to-all-start.14 = ((f32[16,2,4,512]{3,2,1,0:T(4,128)}), f32[16,2,4,512]{3,2,1,0:T(4,128)}, u32[]{:S(2)}, u32[]{:S(2)}) async-start(f32[16,2,4,512]{3,2,1,0:T(4,128)} %get-tuple-element.436), calls=%async_computation.14 | async-start | bytes 524288 | tf_op jit(solution)/shard_map/all_to_all | solution.py:42
  93.0 112.9 %collective-permute-start.16 = (f32[3,400,512]{2,1,0:T(8,128)}, f32[3,400,512]{2,1,0:T(8,128)}, u32[]{:S(2)}, u32[]{:S(2)}) collective-permute-start(f32[3,400,512]{2,1,0:T(8,128)} %bitcast.112), channel_id=1, source_target_pairs={{0,16},{16,0},{1,17},{17,1},{2,18},{18,2},{3,19},{19,3},{4,20},{20... | collective-permute-start | bytes 7372808 | tf_op jit(solution)/shard_map/ppermute | solution.py:1015
  95.1 23.5 %collective-permute-start.15 = (f32[400,512]{1,0:T(8,128)}, f32[400,512]{1,0:T(8,128)S(1)}, u32[]{:S(2)}, u32[]{:S(2)}) collective-permute-start(f32[400,512]{1,0:T(8,128)} %pick_joining.1), channel_id=1, source_target_pairs={{16,0},{17,1},{18,2},{19,3},{20,4},{21,5},{22,6},{23,7},{24,8},{25... | collective-permute-start | bytes 2457608 | tf_op jit(solution)/shard_map/ppermute | solution.py:1057
  106.6 12.0 %all-to-all-start.15 = ((f32[16,2,2,512]{3,2,1,0:T(2,128)}), f32[16,2,2,512]{3,2,1,0:T(2,128)}, u32[]{:S(2)}, u32[]{:S(2)}) async-start(f32[16,2,2,512]{3,2,1,0:T(2,128)} %get-tuple-element.438), calls=%async_computation.15 | async-start | bytes 262144 | tf_op jit(solution)/shard_map/all_to_all | solution.py:42
  125.6 14.1 %all-to-all-start.16 = ((f32[16,2,2,640]{3,2,1,0:T(2,128)}), f32[16,2,2,640]{3,2,1,0:T(2,128)}, u32[]{:S(2)}, u32[]{:S(2)}) async-start(f32[16,2,2,640]{3,2,1,0:T(2,128)} %get-tuple-element.444), calls=%async_computation.16 | async-start | bytes 327680 | tf_op jit(solution)/shard_map/all_to_all | solution.py:42
  132.5 63.9 %copy-start.48 = (s32[6]{0:T(128)}, s32[6]{0:T(128)S(1)}, u32[]{:S(2)}) copy-start(s32[6]{0:T(128)S(1)} %pad_add_fusion.2.meta) | copy-start | bytes 76
  139.3 57.1 %copy-start.15 = (f32[6,512]{1,0:T(8,128)}, f32[6,512]{1,0:T(8,128)S(1)}, u32[]{:S(2)}) copy-start(f32[6,512]{1,0:T(8,128)S(1)} %get-tuple-element.572.refs_3_.refs_4_.refs_6_.refs_7_) | copy-start | bytes 36868
  145.6 14.5 %all-to-all-start.17 = ((f32[16,2,2,512]{3,2,1,0:T(2,128)}), f32[16,2,2,512]{3,2,1,0:T(2,128)}, u32[]{:S(2)}, u32[]{:S(2)}) async-start(f32[16,2,2,512]{3,2,1,0:T(2,128)} %get-tuple-element.446), calls=%async_computation.17 | async-start | bytes 262144 | tf_op jit(solution)/shard_map/all_to_all | solution.py:42
  165.9 12.0 %all-to-all-start.18 = ((f32[16,2,2,512]{3,2,1,0:T(2,128)}), f32[16,2,2,512]{3,2,1,0:T(2,128)}, u32[]{:S(2)}, u32[]{:S(2)}) async-start(f32[16,2,2,512]{3,2,1,0:T(2,128)} %get-tuple-element.449), calls=%async_computation.18 | async-start | bytes 262144 | tf_op jit(solution)/shard_map/all_to_all | solution.py:42
  202.3 11.3 %all-to-all-start.20 = ((f32[16,2,2,512]{3,2,1,0:T(2,128)}), f32[16,2,2,512]{3,2,1,0:T(2,128)S(1)}, u32[]{:S(2)}, u32[]{:S(2)}) async-start(f32[16,2,2,512]{3,2,1,0:T(2,128)} %get-tuple-element.455), calls=%async_computation.20 | async-start | bytes 262144 | tf_op jit(solution)/shard_map/all_to_all | solution.py:42
  244.0 11.5 %all-to-all-start.22 = ((f32[16,2,2,512]{3,2,1,0:T(2,128)}), f32[16,2,2,512]{3,2,1,0:T(2,128)S(1)}, u32[]{:S(2)}, u32[]{:S(2)}) async-start(f32[16,2,2,512]{3,2,1,0:T(2,128)} %get-tuple-element.467), calls=%async_computation.22 | async-start | bytes 262144 | tf_op jit(solution)/shard_map/all_to_all | solution.py:42
  264.0 19.0 %all-to-all-start.23 = ((f32[16,2,2,512]{3,2,1,0:T(2,128)}), f32[16,2,2,512]{3,2,1,0:T(2,128)S(1)}, u32[]{:S(2)}, u32[]{:S(2)}) async-start(f32[16,2,2,512]{3,2,1,0:T(2,128)} %get-tuple-element.473), calls=%async_computation.23 | async-start | bytes 262144 | tf_op jit(solution)/shard_map/all_to_all | solution.py:42
  269.3 149.1 %all-reduce.6.cloned.1.call-start = ((), (), s32[]{:S(2)}) async-start(), calls=%async_computation.24 | async-start | bytes 3145728 | tf_op jit(solution)/shard_map/psum | solution.py:1117
  283.0 8.5 %collective-permute-start.17 = (f32[768,512]{1,0:T(8,128)}, f32[768,512]{1,0:T(8,128)}, u32[]{:S(2)}, u32[]{:S(2)}) collective-permute-start(f32[768,512]{1,0:T(8,128)} %get-tuple-element.490), channel_id=1, source_target_pairs={{0,16},{16,0},{1,17},{17,1},{2,18},{18,2},{3,19},{19,3},{4,20},{20... | collective-permute-start | bytes 4718600 | tf_op jit(solution)/shard_map/ppermute | solution.py:1015
  294.9 309.3 %all-reduce.8.cloned.1.call-start = ((), (), s32[]{:S(2)}) async-start(), calls=%async_computation.25 | async-start | bytes 6815744 | tf_op jit(solution)/shard_map/psum | solution.py:1140
  295.1 17.6 %all-to-all-start = ((f32[16,2,2,512]{3,2,1,0:T(2,128)}), f32[16,2,2,512]{3,2,1,0:T(2,128)S(1)}, u32[]{:S(2)}, u32[]{:S(2)}) async-start(f32[16,2,2,512]{3,2,1,0:T(2,128)} %get-tuple-element.171), calls=%async_computation | async-start | bytes 262144 | tf_op jit(solution)/shard_map/cond/branch_1_fun/all_to_all | solution.py:42
  321.5 12.8 %all-to-all-start.1 = ((f32[16,2,2,512]{3,2,1,0:T(2,128)}), f32[16,2,2,512]{3,2,1,0:T(2,128)S(1)}, u32[]{:S(2)}, u32[]{:S(2)}) async-start(f32[16,2,2,512]{3,2,1,0:T(2,128)} %get-tuple-element.185), calls=%async_computation.1 | async-start | bytes 262144 | tf_op jit(solution)/shard_map/cond/branch_1_fun/all_to_all | solution.py:42
  344.5 13.8 %all-to-all-start.2 = ((f32[16,2,4,512]{3,2,1,0:T(4,128)}), f32[16,2,4,512]{3,2,1,0:T(4,128)}, u32[]{:S(2)}, u32[]{:S(2)}) async-start(f32[16,2,4,512]{3,2,1,0:T(4,128)} %get-tuple-element.218), calls=%async_computation.2 | async-start | bytes 524288 | tf_op jit(solution)/shard_map/cond/branch_1_fun/all_to_all | solution.py:42
  365.4 12.2 %all-to-all-start.3 = ((f32[16,2,2,512]{3,2,1,0:T(2,128)}), f32[16,2,2,512]{3,2,1,0:T(2,128)}, u32[]{:S(2)}, u32[]{:S(2)}) async-start(f32[16,2,2,512]{3,2,1,0:T(2,128)} %get-tuple-element.225), calls=%async_computation.3 | async-start | bytes 262144 | tf_op jit(solution)/shard_map/cond/branch_1_fun/all_to_all | solution.py:42
  377.6 36.3 %collective-permute-start = (f32[896,512]{1,0:T(8,128)}, f32[896,512]{1,0:T(8,128)}, u32[]{:S(2)}, u32[]{:S(2)}) collective-permute-start(f32[896,512]{1,0:T(8,128)} %get-tuple-element.234), channel_id=1, source_target_pairs={{0,16},{16,0},{1,17},{17,1},{2,18},{18,2},{3,19},{19,3},{4,20},{20... | collective-permute-start | bytes 5505032 | tf_op jit(solution)/shard_map/cond/branch_1_fun/ppermute | solution.py:1015
  385.4 17.6 %all-to-all-start.4 = ((f32[16,2,2,512]{3,2,1,0:T(2,128)}), f32[16,2,2,512]{3,2,1,0:T(2,128)S(1)}, u32[]{:S(2)}, u32[]{:S(2)}) async-start(f32[16,2,2,512]{3,2,1,0:T(2,128)} %get-tuple-element.243), calls=%async_computation.4 | async-start | bytes 262144 | tf_op jit(solution)/shard_map/cond/branch_1_fun/all_to_all | solution.py:42
  403.0 8.4 %collective-permute-start.1 = (f32[768,512]{1,0:T(8,128)}, f32[768,512]{1,0:T(8,128)}, u32[]{:S(2)}, u32[]{:S(2)}) collective-permute-start(f32[768,512]{1,0:T(8,128)} %get-tuple-element.250), channel_id=1, source_target_pairs={{0,16},{16,0},{1,17},{17,1},{2,18},{18,2},{3,19},{19,3},{4,20},{20... | collective-permute-start | bytes 4718600 | tf_op jit(solution)/shard_map/cond/branch_1_fun/ppermute | solution.py:1015
  419.2 14.7 %all-to-all-start.5 = ((f32[16,2,2,512]{3,2,1,0:T(2,128)}), f32[16,2,2,512]{3,2,1,0:T(2,128)S(1)}, u32[]{:S(2)}, u32[]{:S(2)}) async-start(f32[16,2,2,512]{3,2,1,0:T(2,128)} %get-tuple-element.261), calls=%async_computation.5 | async-start | bytes 262144 | tf_op jit(solution)/shard_map/cond/branch_1_fun/all_to_all | solution.py:42
  442.6 15.5 %all-to-all-start.6 = ((f32[16,2,2,512]{3,2,1,0:T(2,128)}), f32[16,2,2,512]{3,2,1,0:T(2,128)S(1)}, u32[]{:S(2)}, u32[]{:S(2)}) async-start(f32[16,2,2,512]{3,2,1,0:T(2,128)} %get-tuple-element.275), calls=%async_computation.6 | async-start | bytes 262144 | tf_op jit(solution)/shard_map/cond/branch_1_fun/all_to_all | solution.py:42
  472.6 4.0 collective-permute-start.2
  479.8 33.6 %collective-permute-start.4 = (f32[2,400,512]{2,1,0:T(8,128)}, f32[2,400,512]{2,1,0:T(8,128)}, u32[]{:S(2)}, u32[]{:S(2)}) collective-permute-start(f32[2,400,512]{2,1,0:T(8,128)} %get-tuple-element.293), channel_id=1, source_target_pairs={{0,16},{1,17},{2,18},{3,19},{4,20},{5,21},{6,22},{7,23},{8,24},{9,... | collective-permute-start | bytes 4915208 | tf_op jit(solution)/shard_map/cond/branch_1_fun/ppermute | solution.py:1056
  483.0 34.2 %collective-permute-start.7 = (f32[768,512]{1,0:T(8,128)}, f32[768,512]{1,0:T(8,128)}, u32[]{:S(2)}, u32[]{:S(2)}) collective-permute-start(f32[768,512]{1,0:T(8,128)} %get-tuple-element.300), channel_id=1, source_target_pairs={{0,16},{1,17},{2,18},{3,19},{4,20},{5,21},{6,22},{7,23},{8,24},{9,... | collective-permute-start | bytes 4718600 | tf_op jit(solution)/shard_map/cond/branch_1_fun/ppermute | solution.py:1056
  485.5 26.9 %all-to-all-start.7 = ((f32[4,224,512]{2,1,0:T(8,128)}), f32[4,224,512]{2,1,0:T(8,128)S(1)}, u32[]{:S(2)}, u32[]{:S(2)}) async-start(f32[4,224,512]{2,1,0:T(8,128)} %bitcast.117), calls=%async_computation.7 | async-start | bytes 3670016 | tf_op jit(solution)/shard_map/cond/branch_1_fun/all_to_all | solution.py:47
  489.2 18.7 %collective-permute-start.6 = (f32[2,200,512]{2,1,0:T(8,128)}, f32[2,200,512]{2,1,0:T(8,128)}, u32[]{:S(2)}, u32[]{:S(2)}) collective-permute-start(f32[2,200,512]{2,1,0:T(8,128)} %get-tuple-element.295), channel_id=1, source_target_pairs={{0,16},{1,17},{2,18},{3,19},{4,20},{5,21},{6,22},{7,23},{8,24},{9,... | collective-permute-start | bytes 2457608 | tf_op jit(solution)/shard_map/cond/branch_1_fun/ppermute | solution.py:1056
  493.5 15.8 %collective-permute-start.5 = (f32[1,400,512]{2,1,0:T(8,128)}, f32[1,400,512]{2,1,0:T(8,128)}, u32[]{:S(2)}, u32[]{:S(2)}) collective-permute-start(f32[1,400,512]{2,1,0:T(8,128)} %slice.121), channel_id=1, source_target_pairs={{16,0},{17,1},{18,2},{19,3},{20,4},{21,5},{22,6},{23,7},{24,8},{25... | collective-permute-start | bytes 2457608 | tf_op jit(solution)/shard_map/cond/branch_1_fun/ppermute | solution.py:1057
  496.9 16.5 %collective-permute-start.3 = (f32[1,200,512]{2,1,0:T(8,128)}, f32[1,200,512]{2,1,0:T(8,128)}, u32[]{:S(2)}, u32[]{:S(2)}) collective-permute-start(f32[1,200,512]{2,1,0:T(8,128)} %slice.119), channel_id=1, source_target_pairs={{16,0},{17,1},{18,2},{19,3},{20,4},{21,5},{22,6},{23,7},{24,8},{25... | collective-permute-start | bytes 1228808 | tf_op jit(solution)/shard_map/cond/branch_1_fun/ppermute | solution.py:1057
  604.2 8.9 %collective-permute-start.18 = (f32[1664,512]{1,0:T(8,128)}, f32[1664,512]{1,0:T(8,128)S(1)}, u32[]{:S(2)}, u32[]{:S(2)}) collective-permute-start(f32[1664,512]{1,0:T(8,128)} %all-reduce.8.cloned.1.call-done), channel_id=1, source_target_pairs={{0,16},{16,0},{1,17},{17,1},{2,18},{18,2},{3,19},{19,3},{4,20},{20... | collective-permute-start | bytes 10223624 | tf_op jit(solution)/shard_map/ppermute | solution.py:1015
  604.3 8.8 %collective-permute-start.19 = (f32[896,512]{1,0:T(8,128)}, f32[896,512]{1,0:T(8,128)S(1)}, u32[]{:S(2)}, u32[]{:S(2)}) collective-permute-start(f32[896,512]{1,0:T(8,128)} %get-tuple-element.516), channel_id=1, source_target_pairs={{16,0},{17,1},{18,2},{19,3},{20,4},{21,5},{22,6},{23,7},{24,8},{25... | collective-permute-start | bytes 5505032 | tf_op jit(solution)/shard_map/ppermute | solution.py:1057
  (63 other events, 609.6 us)
Sparse Core Ops, SparseCore 0:
  295.1 122.6 all-reduce.5
  425.0 179.2 all-reduce.7

commit v2 on v1

--- a/solution.py
+++ b/solution.py
@@ -1077,10 +1077,7 @@
     both = jnp.concatenate([length, half_len, flag, half_len, join_len, flag, picks[MB - 1 :]])
 
     def small(block):
-        own, far = taps, far_taps
-        if block:
-            own, far, _ = lax.optimization_barrier((taps, far_taps, c14.z[3]))
-        t = jnp.where(first == (block == 0), own, far)
+        t = jnp.where(first == (block == 0), taps, far_taps)
         return t[: 5 * TAPS].reshape(5, TAPS, C), t[5 * TAPS : 5 * TAPS + 6], t[5 * TAPS + 6 :]
 
     excitations = split_squeeze(meta1, squeeze, far_squeeze)
@@ -1096,7 +1093,7 @@
     c14 = Block(False, meta1, small(0), {**parts0[0][1], **parts0[1][1]}, stages)
     c14.x, c14.x_far, c14.first_matrix = inputs, far_rows, (pw[0], far_w0)
     c14.excitation = excitations[0]
-    c14.forward({1: excitations[0], 2: (parts0[1][0],)})
+    c14.forward({2: (parts0[1][0],)})
     late_picks, _ = lax.optimization_barrier((picks, c14.z[3]))
     far_joining = to_lower(pick_joining(late_picks, features.reshape(MB, 2, HALF, C)))
     c15 = Block(True, meta2, small(1), {**parts1[0][1], **parts1[1][1], **parts1[2][1]}, stages)
@@ -1164,7 +1161,8 @@
     block_out, dx, came0, sum3 = fenced(always, ending, half12)
     came3 = to_lower(sum3)
     sum12, _ = lax.optimization_barrier((sum12, sum3))
-    came12 = swap(sum12)
+    spare = sum12.shape[0] - PIECE_ROWS[1]
+    came12 = swap(lax.dynamic_slice_in_dim(sum12, jnp.where(first, 0, spare), PIECE_ROWS[1]))
     split, lead = PIECE_ROWS[1], 3 * C // 2
 
     def assembled(rest_top, rest_bottom, lead_top, lead_bottom):
@@ -1176,8 +1174,8 @@
 
     pw_grad, res_grad, rows = lax.cond(
         first,
-        lambda s3, c3, s12, c12, s0, c0: assembled(s3, c3, s12[split:], c12[split:]),
-        lambda s3, c3, s12, c12, s0, c0: assembled(c12[:split], s12[:split], c0, s0),
+        lambda s3, c3, s12, c12, s0, c0: assembled(s3, c3, s12[split:], c12[split - spare :]),
+        lambda s3, c3, s12, c12, s0, c0: assembled(c12, s12[:split], c0, s0),
         sum3, came3, sum12, came12, sum0, came0,
     )
     dw_grad = rows[TAIL_ROWS : TAIL_ROWS + 40].reshape(1, 5, 8, C)

time: 644 us -> 638 us (level)
    ppermute x4, waiting for transfers between devices: 7.53 us -> 0.01 us  [per_device(): to_lower = lambda x: lax.ppermute(x, 'section', [(1, 0)])]
where the time goes in v2:
time: 638 us; the launch traced here: 626 us
  Pallas kernels  257 us (40%)
  starting transfers between devices  116 us (18%)
  blocking collectives  102 us (16%)
  waiting for transfers between devices  68.1 us (11%)
  local copies, waits for them, and re-layouts  31.3 us (5%)
  other arithmetic  30.1 us (5%)
  between operations  15.9 us (2%)
  loops' own time  6.75 us (1%)
    pallas_call x42, Pallas kernels, call(): pl.pallas_call(inner, out_shape=shapes, grid_spec=pltpu.PrefetchScalarGri...  257 us
    all_to_all x18, starting transfers between devices, exchange(): return lax.all_to_all(block, 'dp', 0, 0)  93 us
    all_to_all x3, blocking collectives, exchange(): return lax.all_to_all(block, 'dp', 0, 0, axis_index_groups=groups)  76.2 us
    all_to_all x18, waiting for transfers between devices, exchange(): return lax.all_to_all(block, 'dp', 0, 0)  47.7 us
    all_to_all x2, blocking collectives, exchange(): return lax.all_to_all(block, 'dp', 0, 0)  25.4 us
  transfers between devices with their start and end apart: 41, of which 20 were waited for; matrix products, arithmetic and copies ran while one was open for 7% of the time, Pallas kernels for 35%

profile of v2, /device:TPU:0, one launch (start us, length us, event | category | flops | bytes accessed | tf_op | source)
XLA Modules:
  0.0 626.3 jit_solution(7856260702091380723)
XLA Ops:
  20.3 5.6 c14_forward_0.1
  25.9 7.9 %all-to-all-start.11 = ((f32[16,2,2,640]{3,2,1,0:T(2,128)}), f32[16,2,2,640]{3,2,1,0:T(2,128)}, u32[]{:S(2)}, u32[]{:S(2)}) async-start(f32[16,2,2,640]{3,2,1,0:T(2,128)} %get-tuple-element.422), calls=%async_computation.11 | async-start | bytes 327680 | tf_op jit(solution)/shard_map/all_to_all | solution.py:42
  42.2 5.9 c14_forward_1.1
  60.0 5.9 c14_forward_2.1
  78.9 5.9 c14_forward_3.1
  116.3 6.9 %c14_tail_c15_forward_0.1 = (f32[2,400,512]{2,1,0:T(8,128)}, f32[2,2,512]{2,1,0:T(2,128)}, f32[2,2,512]{2,1,0:T(2,128)}, f32[2,8,512]{2,1,0:T(8,128)}, f32[2,64,...) custom-call(s32[11]{0:T(128)S(1)} %concatenate.78.meta, ...), custom_call_target="tpu_custom_call" | custom-call | flops 1258291200 | bytes 10297600 | tf_op jit(solution)/shard_map/c14_tail_c15_forward_0/pallas_call | solution.py:211
  123.3 7.1 %all-to-all-start.16 = ((f32[16,2,2,640]{3,2,1,0:T(2,128)}), f32[16,2,2,640]{3,2,1,0:T(2,128)}, u32[]{:S(2)}, u32[]{:S(2)}) async-start(f32[16,2,2,640]{3,2,1,0:T(2,128)} %get-tuple-element.440), calls=%async_computation.16 | async-start | bytes 327680 | tf_op jit(solution)/shard_map/all_to_all | solution.py:42
  131.9 6.0 prepare_1_1.1.refs_5_.refs_6_.refs_7_.refs_2_
  138.3 5.8 c15_forward_1.1
  144.1 6.6 %all-to-all-start.17 = ((f32[16,2,2,512]{3,2,1,0:T(2,128)}), f32[16,2,2,512]{3,2,1,0:T(2,128)}, u32[]{:S(2)}, u32[]{:S(2)}) async-start(f32[16,2,2,512]{3,2,1,0:T(2,128)} %get-tuple-element.442), calls=%async_computation.17 | async-start | bytes 262144 | tf_op jit(solution)/shard_map/all_to_all | solution.py:42
  158.6 5.8 c15_forward_2.1
  176.4 5.8 c15_forward_3.1
  182.3 12.7 %all_to_all.112.refs_1_.refs_3_ = f32[16,2,4,512]{3,2,1,0:T(4,128)} all-to-all(f32[16,2,4,512]{3,2,1,0:T(4,128)} %get-tuple-element.449), channel_id=1, replica_groups=mesh['section'=2,'dp'=16] {'dp'}, dimensions={0} | all-to-all | bytes 524288 | tf_op jit(solution)/shard_map/all_to_all | solution.py:42
  195.0 5.8 c15_forward_4.1
  204.3 7.8 %all-to-all-done.20.refs_1_ = f32[16,2,2,512]{3,2,1,0:T(2,128)S(1)} async-done(((f32[16,2,2,512]{3,2,1,0:T(2,128)}), f32[16,2,2,512]{3,2,1,0:T(2,128)S(1)}, u32[]{:S(2)}, u32[]{:S(2)}) %all-to-all-start.20) | async-done | bytes 131104 | tf_op jit(solution)/shard_map/all_to_all | solution.py:42
  212.7 8.7 %c15_tail.1 = (f32[2,400,512]{2,1,0:T(8,128)}, f32[2,2,512]{2,1,0:T(2,128)}, f32[2,2,512]{2,1,0:T(2,128)}, f32[2,8,512]{2,1,0:T(8,128)}, f32[2,64,8]{2,1,0:T(8,1...) custom-call(s32[6]{0:T(128)S(1)} %pad_add_fusion.2.meta, ...), custom_call_target="tpu_custom_call" | custom-call | bytes 14670080 | tf_op jit(solution)/shard_map/c15_tail/pallas_call | solution.py:211
  221.5 12.7 %all_to_all.113.refs_3_.refs_0_ = f32[16,2,4,512]{3,2,1,0:T(4,128)} all-to-all(f32[16,2,4,512]{3,2,1,0:T(4,128)} %get-tuple-element.458), channel_id=1, replica_groups=mesh['section'=2,'dp'=16] {'dp'}, dimensions={0} | all-to-all | bytes 524288 | tf_op jit(solution)/shard_map/all_to_all | solution.py:42
  234.2 7.9 %c15_backward_4.1 = (f32[256,512]{1,0:T(8,128)S(1)}, bf16[2,400,1024]{2,1,0:T(8,128)(2,1)}, f32[2,400,512]{2,1,0:T(8,128)}, f32[16,2,2,512]{3,2,1,0:T(2,128)}) custom-call(s32[6]{0:T(128)S(1)} %pad_add_fusion.2.meta, f32[2,400,512]{2,1,0:T(8,128)} %get-tuple-element.457.refs_0_, ...), custom_call_target="tpu_custom_call", output_to_operand_aliasing={{0}: (12, {})} | custom-call | flops 1258291200 | bytes 11307008 | tf_op jit(solution)/shard_map/c15_backward_4/pallas_call | solution.py:211
  245.8 6.0 c15_weights_4.1
  254.2 7.8 %c15_backward_3.1 = (f32[256,512]{1,0:T(8,128)S(1)}, bf16[2,400,1024]{2,1,0:T(8,128)(2,1)}, f32[2,400,512]{2,1,0:T(8,128)}, f32[16,2,2,512]{3,2,1,0:T(2,128)}) custom-call(s32[6]{0:T(128)S(1)} %pad_add_fusion.2.meta, f32[2,400,512]{2,1,0:T(8,128)} %get-tuple-element.462.refs_0_, ...), custom_call_target="tpu_custom_call", output_to_operand_aliasing={{0}: (13, {})} | custom-call | flops 1258291200 | bytes 12224512 | tf_op jit(solution)/shard_map/c15_backward_3/pallas_call | solution.py:211
  267.3 7.6 %c15_residual_back.1 = (f32[768,512]{1,0:T(8,128)}, f32[768,512]{1,0:T(8,128)}, f32[2,400,512]{2,1,0:T(8,128)}) custom-call(s32[6]{0:T(128)S(1)} %pad_add_fusion.2.meta, f32[16,2,4,512]{3,2,1,0:T(4,128)} %all_to_all.113.refs_3_.refs_0_, f32[2,2,512]{2,1,0:T(2,128)S(1)} %get-tuple-element.443.refs_2_.refs_4_.refs_1_, ...), custom_call_target="tpu_custom_call", output_to_operand_aliasing={{0}: (9, {}), {1}: (10, {})} | custom-call | flops 2516582400 | bytes 12087296 | tf_op jit(solution)/shard_map/c15_residual_back/pallas_call | solution.py:211
  275.0 6.0 c15_weights_3.1
  281.7 8.3 %c15_backward_2.1 = (f32[256,512]{1,0:T(8,128)}, bf16[2,400,1024]{2,1,0:T(8,128)(2,1)}, f32[2,400,512]{2,1,0:T(8,128)}, f32[16,2,2,512]{3,2,1,0:T(2,128)}) custom-call(s32[6]{0:T(128)} %copy-done.50, f32[2,400,512]{2,1,0:T(8,128)} %get-tuple-element.468.refs_0_, ...), custom_call_target="tpu_custom_call", output_to_operand_aliasing={{0}: (13, {})} | custom-call | flops 1258291200 | bytes 12224512 | tf_op jit(solution)/shard_map/c15_backward_2/pallas_call | solution.py:211
  293.6 122.4 %conditional.3 = (f32[2,200,512]{2,1,0:T(8,128)}, f32[1664,512]{1,0:T(8,128)}, f32[2,400,512]{2,1,0:T(8,128)}, f32[2,208,512]{2,1,0:T(8,128)}, bf16[2,400,1024]{...) conditional(s32[]{:T(128)} %bitcast.42, () %tuple.52, (f32[16,2,2,512]{3,2,1,0:T(2,128)}, ...), branch_computations={%region_0.1_spmd, %region_1.2_spmd} | conditional | flops 12685410304 | bytes 178855648 | solution.py:1020
  293.6 7.3 %all-to-all-start = ((f32[16,2,2,512]{3,2,1,0:T(2,128)}), f32[16,2,2,512]{3,2,1,0:T(2,128)S(1)}, u32[]{:S(2)}, u32[]{:S(2)}) async-start(f32[16,2,2,512]{3,2,1,0:T(2,128)} %get-tuple-element.171), calls=%async_computation | async-start | bytes 262144 | tf_op jit(solution)/shard_map/cond/branch_1_fun/all_to_all | solution.py:42
  301.0 6.7 %c15_weights_2.1 = (f32[896,512]{1,0:T(8,128)}, f32[896,512]{1,0:T(8,128)}) custom-call(s32[6]{0:T(128)} %get-tuple-element.167.meta, f32[2,400,512]{2,1,0:T(8,128)} %get-tuple-element.169.refs_0_.refs_1_, f32[2,2,512]{2,1,0:T(2,128)} %get-tuple-element.173.refs_1_.refs_5_, f32[6,512]{1,0:T(8,128)} %get-tuple-element.174.refs_2_.refs_6_, ...), custom_call_target="tpu_custom_call" | custom-call | flops 1258291200 | bytes 7030784 | tf_op jit(solution)/shard_map/cond/branch_1_fun/c15_weights_2/pallas_call | solution.py:211
  312.0 8.1 %c15_backward_1.1 = (f32[256,512]{1,0:T(8,128)S(1)}, bf16[2,400,1024]{2,1,0:T(8,128)(2,1)}, f32[2,400,512]{2,1,0:T(8,128)}, f32[16,2,2,512]{3,2,1,0:T(2,128)}) custom-call(s32[6]{0:T(128)S(1)} %copy-done.51, f32[2,400,512]{2,1,0:T(8,128)} %get-tuple-element.168.refs_0_, ...), custom_call_target="tpu_custom_call", output_to_operand_aliasing={{0}: (14, {})} | custom-call | flops 1258291200 | bytes 12224512 | tf_op jit(solution)/shard_map/cond/branch_1_fun/c15_backward_1/pallas_call | solution.py:211
  324.6 6.0 c15_weights_1.1
  333.1 9.5 %c15_backward_0_c14_tail_back.1 = (f32[256,512]{1,0:T(8,128)S(1)}, bf16[2,400,1024]{2,1,0:T(8,128)(2,1)}, f32[2,200,512]{2,1,0:T(8,128)}, f32[2,200,512]{2,1,0:T...) custom-call(s32[11]{0:T(128)} %get-tuple-element.166.meta, ...), custom_call_target="tpu_custom_call", output_to_operand_aliasing={{0}: (30, {})} | custom-call | flops 1258291200 | bytes 24387840 | tf_op jit(solution)/shard_map/cond/branch_1_fun/c15_backward_0_c14_tail_back/pallas_call | solution.py:211
  347.7 5.7 c15_weights_0.1
  356.5 7.1 %c14_backward_4.1 = (f32[256,512]{1,0:T(8,128)S(1)}, bf16[2,208,1024]{2,1,0:T(8,128)(2,1)}, f32[2,400,512]{2,1,0:T(8,128)}, f32[16,2,2,512]{3,2,1,0:T(2,128)}) custom-call(s32[5]{0:T(128)S(1)} %copy-done.46, f32[2,208,512]{2,1,0:T(8,128)} %get-tuple-element.216.refs_0_, ...), custom_call_target="tpu_custom_call", output_to_operand_aliasing={{0}: (13, {})} | custom-call | flops 654311424 | bytes 9996288 | tf_op jit(solution)/shard_map/cond/branch_1_fun/c14_backward_4/pallas_call | solution.py:211
  368.0 5.6 c14_weights_4.1
  375.9 7.8 %c14_backward_3.1 = (f32[256,512]{1,0:T(8,128)S(1)}, bf16[2,400,1024]{2,1,0:T(8,128)(2,1)}, f32[2,400,512]{2,1,0:T(8,128)}, f32[16,2,2,512]{3,2,1,0:T(2,128)}) custom-call(s32[5]{0:T(128)S(1)} %copy-done.46, f32[2,400,512]{2,1,0:T(8,128)} %get-tuple-element.224.refs_0_, ...), custom_call_target="tpu_custom_call", output_to_operand_aliasing={{0}: (13, {})} | custom-call | flops 1258291200 | bytes 12224512 | tf_op jit(solution)/shard_map/cond/branch_1_fun/c14_backward_3/pallas_call | solution.py:211
  389.2 6.2 c14_residual_back.1
  395.4 6.0 c14_weights_3.1
  401.6 8.2 %c14_backward_2.1 = (f32[256,512]{1,0:T(8,128)}, bf16[2,400,1024]{2,1,0:T(8,128)(2,1)}, f32[2,400,512]{2,1,0:T(8,128)}, f32[16,2,2,512]{3,2,1,0:T(2,128)}) custom-call(s32[5]{0:T(128)} %get-tuple-element.215.meta, f32[2,400,512]{2,1,0:T(8,128)} %get-tuple-element.231.refs_0_, ...), custom_call_target="tpu_custom_call", output_to_operand_aliasing={{0}: (13, {})} | custom-call | flops 1258291200 | bytes 11175936 | tf_op jit(solution)/shard_map/cond/branch_1_fun/c14_backward_2/pallas_call | solution.py:211
  417.0 174.8 %conditional.4 = (f32[768,512]{1,0:T(8,128)}, f32[896,512]{1,0:T(8,128)S(1)}, f32[1,1200,512]{2,1,0:T(8,128)}, f32[1,1200,512]{2,1,0:T(8,128)}) conditional(s32[]{:T(128)} %bitcast.42, () %tuple.51, (f32[16,2,2,512]{3,2,1,0:T(2,128)}, s32[5]{0:T(128)S(1)}, f32[2,400,512]{2,1,0:T(8,128)}, f32[2,2,512]{2,1,0:T(2,128)S(1)}, f32[6,512]{1,0:T(8,128)S(1)}, ...), branch_computations={%region_3.4_spmd, %region_4.10_spmd} | conditional | flops 6300770304 | bytes 133450904 | solution.py:1020
  417.0 6.7 %all-to-all-start.5 = ((f32[16,2,2,512]{3,2,1,0:T(2,128)}), f32[16,2,2,512]{3,2,1,0:T(2,128)S(1)}, u32[]{:S(2)}, u32[]{:S(2)}) async-start(f32[16,2,2,512]{3,2,1,0:T(2,128)} %get-tuple-element.261), calls=%async_computation.5 | async-start | bytes 262144 | tf_op jit(solution)/shard_map/cond/branch_1_fun/all_to_all | solution.py:42
  423.7 6.1 c14_weights_2.1
  432.5 8.1 %c14_backward_1.1 = (f32[256,512]{1,0:T(8,128)S(1)}, bf16[2,400,1024]{2,1,0:T(8,128)(2,1)}, f32[2,400,512]{2,1,0:T(8,128)}, f32[16,2,2,512]{3,2,1,0:T(2,128)}) custom-call(s32[5]{0:T(128)S(1)} %get-tuple-element.255.meta, f32[2,400,512]{2,1,0:T(8,128)} %get-tuple-element.258.refs_0_, ...), custom_call_target="tpu_custom_call", output_to_operand_aliasing={{0}: (14, {})} | custom-call | flops 1258291200 | bytes 11175936 | tf_op jit(solution)/shard_map/cond/branch_1_fun/c14_backward_1/pallas_call | solution.py:211
  445.3 6.1 c14_weights_1.1
  456.5 7.4 %c14_backward_0.1 = (f32[256,512]{1,0:T(8,128)S(1)}, bf16[2,400,1024]{2,1,0:T(8,128)(2,1)}, f32[2,400,512]{2,1,0:T(8,128)}) custom-call(s32[5]{0:T(128)S(1)} %get-tuple-element.255.meta, f32[2,400,512]{2,1,0:T(8,128)} %get-tuple-element.273.refs_0_, f32[2,400,512]{2,1,0:T(8,128)} %get-tuple-element.267.refs_9_.refs_0_.refs_1_, ...), custom_call_target="tpu_custom_call", output_to_operand_aliasing={{0}: (14, {})} | custom-call | flops 1258291200 | bytes 12478464 | tf_op jit(solution)/shard_map/cond/branch_1_fun/c14_backward_0/pallas_call | solution.py:211
  463.9 5.6 c14_weights_0.1
  515.0 19.5 %all_to_all.109 = f32[4,56,512]{2,1,0:T(8,128)S(1)} all-to-all(f32[4,56,512]{2,1,0:T(8,128)S(1)} %bitcast.130), channel_id=1, replica_groups={{0,4,8,12},{1,5,9,13},{2,6,10,14},{3,7,11,15},{16,20,24,28},{17,21,25,2..., dimensions={0} | all-to-all | bytes 917504 | tf_op jit(solution)/shard_map/cond/branch_1_fun/all_to_all | solution.py:47
  534.6 21.7 %all_to_all.110 = f32[4,56,512]{2,1,0:T(8,128)S(1)} all-to-all(f32[4,56,512]{2,1,0:T(8,128)S(1)} %broadcast_in_dim.12), channel_id=1, replica_groups={{0,4,8,12},{1,5,9,13},{2,6,10,14},{3,7,11,15},{16,20,24,28},{17,21,25,2..., dimensions={0} | all-to-all | bytes 917504 | tf_op jit(solution)/shard_map/cond/branch_1_fun/all_to_all | solution.py:47
  556.5 35.0 %all_to_all.111 = f32[4,224,512]{2,1,0:T(8,128)S(1)} all-to-all(f32[4,224,512]{2,1,0:T(8,128)S(1)} %broadcast_in_dim.20), channel_id=1, replica_groups={{0,1,2,3},{4,5,6,7},{8,9,10,11},{12,13,14,15},{16,17,18,19},{20,21,22,2..., dimensions={0} | all-to-all | bytes 3670016 | tf_op jit(solution)/shard_map/cond/branch_1_fun/all_to_all | solution.py:47
  593.1 10.1 %all-reduce.8.cloned.1.call-done = f32[1664,512]{1,0:T(8,128)} async-done(((f32[1664,512]{1,0:T(8,128)}), f32[1664,512]{1,0:T(8,128)}) %all-reduce.8.cloned.1.call-update) | async-done | bytes 3407888 | tf_op jit(solution)/shard_map/psum | solution.py:1137
  608.8 6.3 conditional.5
  (295 shorter events, 226.8 us)
Async XLA Ops:
  7.2 26.7 %collective-permute-start.12 = (f32[5,512,512]{2,1,0:T(8,128)}, f32[5,512,512]{2,1,0:T(8,128)}, u32[]{:S(2)}, u32[]{:S(2)}) collective-permute-start(f32[5,512,512]{2,1,0:T(8,128)} %bitcast.103), channel_id=1, source_target_pairs={{0,16},{16,0},{1,17},{17,1},{2,18},{18,2},{3,19},{19,3},{4,20},{20... | collective-permute-start | bytes 15728648 | tf_op jit(solution)/shard_map/ppermute | solution.py:1015
  7.7 7.8 %collective-permute-start.8 = (s32[3]{0:T(128)}, s32[3]{0:T(128)S(1)}, u32[]{:S(2)}, u32[]{:S(2)}) collective-permute-start(s32[3]{0:T(128)} %bitcast.137), channel_id=1, source_target_pairs={{0,16},{16,0},{1,17},{17,1},{2,18},{18,2},{3,19},{19,3},{4,20},{20... | collective-permute-start | bytes 44 | tf_op jit(solution)/shard_map/ppermute | solution.py:1015
  9.9 10.3 %collective-permute-start.9 = (f32[400,512]{1,0:T(8,128)}, f32[400,512]{1,0:T(8,128)S(1)}, u32[]{:S(2)}, u32[]{:S(2)}) collective-permute-start(f32[400,512]{1,0:T(8,128)} %slice_bitcast_fusion.5), channel_id=1, source_target_pairs={{0,16},{1,17},{2,18},{3,19},{4,20},{5,21},{6,22},{7,23},{8,24},{9,... | collective-permute-start | bytes 2457608 | tf_op jit(solution)/shard_map/ppermute | solution.py:1056
  14.7 5.6 collective-permute-start.11
  14.9 3.8 collective-permute-start.10
  15.5 36.1 %collective-permute-start.13 = (f32[512,512]{1,0:T(8,128)}, f32[512,512]{1,0:T(8,128)}, u32[]{:S(2)}, u32[]{:S(2)}) collective-permute-start(f32[512,512]{1,0:T(8,128)} %bitcast.123), channel_id=1, source_target_pairs={{0,16},{16,0},{1,17},{17,1},{2,18},{18,2},{3,19},{19,3},{4,20},{20... | collective-permute-start | bytes 3145736 | tf_op jit(solution)/shard_map/ppermute | solution.py:1015
  16.9 92.6 %copy-start.57 = (s32[2]{0:T(128)}, s32[2]{0:T(128)S(1)}, u32[]{:S(2)}) copy-start(s32[2]{0:T(128)S(1)} %get-tuple-element.551) | copy-start | bytes 28
  17.0 80.6 %copy-start.43 = (s32[5]{0:T(128)}, s32[5]{0:T(128)S(1)}, u32[]{:S(2)}) copy-start(s32[5]{0:T(128)S(1)} %pad_add_fusion.3.meta) | copy-start | bytes 64
  25.9 16.4 %all-to-all-start.11 = ((f32[16,2,2,640]{3,2,1,0:T(2,128)}), f32[16,2,2,640]{3,2,1,0:T(2,128)}, u32[]{:S(2)}, u32[]{:S(2)}) async-start(f32[16,2,2,640]{3,2,1,0:T(2,128)} %get-tuple-element.422), calls=%async_computation.11 | async-start | bytes 327680 | tf_op jit(solution)/shard_map/all_to_all | solution.py:42
  33.8 82.4 %copy-start.20 = (f32[6,512]{1,0:T(8,128)}, f32[6,512]{1,0:T(8,128)S(1)}, u32[]{:S(2)}) copy-start(f32[6,512]{1,0:T(8,128)S(1)} %get-tuple-element.572.refs_3_.refs_4_.refs_6_) | copy-start | bytes 36868
  48.1 11.3 %all-to-all-start.12 = ((f32[16,2,2,512]{3,2,1,0:T(2,128)}), f32[16,2,2,512]{3,2,1,0:T(2,128)S(1)}, u32[]{:S(2)}, u32[]{:S(2)}) async-start(f32[16,2,2,512]{3,2,1,0:T(2,128)} %get-tuple-element.424), calls=%async_computation.12 | async-start | bytes 262144 | tf_op jit(solution)/shard_map/all_to_all | solution.py:42
  65.9 12.3 %all-to-all-start.13 = ((f32[16,2,2,512]{3,2,1,0:T(2,128)}), f32[16,2,2,512]{3,2,1,0:T(2,128)S(1)}, u32[]{:S(2)}, u32[]{:S(2)}) async-start(f32[16,2,2,512]{3,2,1,0:T(2,128)} %get-tuple-element.427), calls=%async_computation.13 | async-start | bytes 262144 | tf_op jit(solution)/shard_map/all_to_all | solution.py:42
  84.8 12.9 %all-to-all-start.14 = ((f32[16,2,4,512]{3,2,1,0:T(4,128)}), f32[16,2,4,512]{3,2,1,0:T(4,128)}, u32[]{:S(2)}, u32[]{:S(2)}) async-start(f32[16,2,4,512]{3,2,1,0:T(4,128)} %get-tuple-element.430), calls=%async_computation.14 | async-start | bytes 524288 | tf_op jit(solution)/shard_map/all_to_all | solution.py:42
  90.6 25.6 %collective-permute-start.15 = (f32[400,512]{1,0:T(8,128)}, f32[400,512]{1,0:T(8,128)S(1)}, u32[]{:S(2)}, u32[]{:S(2)}) collective-permute-start(f32[400,512]{1,0:T(8,128)} %pick_joining.1), channel_id=1, source_target_pairs={{16,0},{17,1},{18,2},{19,3},{20,4},{21,5},{22,6},{23,7},{24,8},{25... | collective-permute-start | bytes 2457608 | tf_op jit(solution)/shard_map/ppermute | solution.py:1057
  92.7 17.6 %collective-permute-start.14 = (f32[130,512]{1,0:T(8,128)}, f32[130,512]{1,0:T(8,128)}, u32[]{:S(2)}, u32[]{:S(2)}) collective-permute-start(f32[130,512]{1,0:T(8,128)} %select_maximum_fusion.3.refs_0_), channel_id=1, source_target_pairs={{0,16},{16,0},{1,17},{17,1},{2,18},{18,2},{3,19},{19,3},{4,20},{20... | collective-permute-start | bytes 798728 | tf_op jit(solution)/shard_map/ppermute | solution.py:1015
  93.9 110.5 %collective-permute-start.16 = (f32[3,400,512]{2,1,0:T(8,128)}, f32[3,400,512]{2,1,0:T(8,128)}, u32[]{:S(2)}, u32[]{:S(2)}) collective-permute-start(f32[3,400,512]{2,1,0:T(8,128)} %bitcast.112), channel_id=1, source_target_pairs={{0,16},{16,0},{1,17},{17,1},{2,18},{18,2},{3,19},{19,3},{4,20},{20... | collective-permute-start | bytes 7372808 | tf_op jit(solution)/shard_map/ppermute | solution.py:1015
  102.8 13.4 %all-to-all-start.15 = ((f32[16,2,2,512]{3,2,1,0:T(2,128)}), f32[16,2,2,512]{3,2,1,0:T(2,128)}, u32[]{:S(2)}, u32[]{:S(2)}) async-start(f32[16,2,2,512]{3,2,1,0:T(2,128)} %get-tuple-element.432), calls=%async_computation.15 | async-start | bytes 262144 | tf_op jit(solution)/shard_map/all_to_all | solution.py:42
  123.3 15.0 %all-to-all-start.16 = ((f32[16,2,2,640]{3,2,1,0:T(2,128)}), f32[16,2,2,640]{3,2,1,0:T(2,128)}, u32[]{:S(2)}, u32[]{:S(2)}) async-start(f32[16,2,2,640]{3,2,1,0:T(2,128)} %get-tuple-element.440), calls=%async_computation.16 | async-start | bytes 327680 | tf_op jit(solution)/shard_map/all_to_all | solution.py:42
  131.1 143.9 %copy-start.50 = (s32[6]{0:T(128)}, s32[6]{0:T(128)S(1)}, u32[]{:S(2)}) copy-start(s32[6]{0:T(128)S(1)} %pad_add_fusion.2.meta) | copy-start | bytes 76
  131.9 143.1 %copy-start.23 = (f32[6,512]{1,0:T(8,128)}, f32[6,512]{1,0:T(8,128)S(1)}, u32[]{:S(2)}) copy-start(f32[6,512]{1,0:T(8,128)S(1)} %get-tuple-element.571.refs_2_.refs_3_.refs_5_.refs_6_) | copy-start | bytes 36868
  131.9 143.1 %copy-start.25 = (f32[6,512]{1,0:T(8,128)}, f32[6,512]{1,0:T(8,128)S(1)}, u32[]{:S(2)}) copy-start(f32[6,512]{1,0:T(8,128)S(1)} %get-tuple-element.570.refs_3_.refs_4_.refs_6_.refs_7_) | copy-start | bytes 36868
  144.1 123.2 %copy-start.31 = (f32[2,2,512]{2,1,0:T(2,128)}, f32[2,2,512]{2,1,0:T(2,128)S(1)}, u32[]{:S(2)}) copy-start(f32[2,2,512]{2,1,0:T(2,128)S(1)} %get-tuple-element.443.refs_2_.refs_4_.refs_1_) | copy-start | bytes 24580
  144.1 14.5 %all-to-all-start.17 = ((f32[16,2,2,512]{3,2,1,0:T(2,128)}), f32[16,2,2,512]{3,2,1,0:T(2,128)}, u32[]{:S(2)}, u32[]{:S(2)}) async-start(f32[16,2,2,512]{3,2,1,0:T(2,128)} %get-tuple-element.442), calls=%async_computation.17 | async-start | bytes 262144 | tf_op jit(solution)/shard_map/all_to_all | solution.py:42
  164.4 12.0 %all-to-all-start.18 = ((f32[16,2,2,512]{3,2,1,0:T(2,128)}), f32[16,2,2,512]{3,2,1,0:T(2,128)}, u32[]{:S(2)}, u32[]{:S(2)}) async-start(f32[16,2,2,512]{3,2,1,0:T(2,128)} %get-tuple-element.445), calls=%async_computation.18 | async-start | bytes 262144 | tf_op jit(solution)/shard_map/all_to_all | solution.py:42
  200.8 11.3 %all-to-all-start.20 = ((f32[16,2,2,512]{3,2,1,0:T(2,128)}), f32[16,2,2,512]{3,2,1,0:T(2,128)S(1)}, u32[]{:S(2)}, u32[]{:S(2)}) async-start(f32[16,2,2,512]{3,2,1,0:T(2,128)} %get-tuple-element.451), calls=%async_computation.20 | async-start | bytes 262144 | tf_op jit(solution)/shard_map/all_to_all | solution.py:42
  242.1 11.5 %all-to-all-start.22 = ((f32[16,2,2,512]{3,2,1,0:T(2,128)}), f32[16,2,2,512]{3,2,1,0:T(2,128)S(1)}, u32[]{:S(2)}, u32[]{:S(2)}) async-start(f32[16,2,2,512]{3,2,1,0:T(2,128)} %get-tuple-element.463), calls=%async_computation.22 | async-start | bytes 262144 | tf_op jit(solution)/shard_map/all_to_all | solution.py:42
  262.0 19.0 %all-to-all-start.23 = ((f32[16,2,2,512]{3,2,1,0:T(2,128)}), f32[16,2,2,512]{3,2,1,0:T(2,128)S(1)}, u32[]{:S(2)}, u32[]{:S(2)}) async-start(f32[16,2,2,512]{3,2,1,0:T(2,128)} %get-tuple-element.469), calls=%async_computation.23 | async-start | bytes 262144 | tf_op jit(solution)/shard_map/all_to_all | solution.py:42
  267.3 148.9 %all-reduce.6.cloned.1.call-start = ((), (), s32[]{:S(2)}) async-start(), calls=%async_computation.24 | async-start | bytes 3145728 | tf_op jit(solution)/shard_map/psum | solution.py:1114
  281.0 9.0 %collective-permute-start.17 = (f32[768,512]{1,0:T(8,128)}, f32[768,512]{1,0:T(8,128)}, u32[]{:S(2)}, u32[]{:S(2)}) collective-permute-start(f32[768,512]{1,0:T(8,128)} %get-tuple-element.486), channel_id=1, source_target_pairs={{0,16},{16,0},{1,17},{17,1},{2,18},{18,2},{3,19},{19,3},{4,20},{20... | collective-permute-start | bytes 4718600 | tf_op jit(solution)/shard_map/ppermute | solution.py:1015
  292.9 310.2 %all-reduce.8.cloned.1.call-start = ((), (), s32[]{:S(2)}) async-start(), calls=%async_computation.25 | async-start | bytes 6815744 | tf_op jit(solution)/shard_map/psum | solution.py:1137
  293.6 17.6 %all-to-all-start = ((f32[16,2,2,512]{3,2,1,0:T(2,128)}), f32[16,2,2,512]{3,2,1,0:T(2,128)S(1)}, u32[]{:S(2)}, u32[]{:S(2)}) async-start(f32[16,2,2,512]{3,2,1,0:T(2,128)} %get-tuple-element.171), calls=%async_computation | async-start | bytes 262144 | tf_op jit(solution)/shard_map/cond/branch_1_fun/all_to_all | solution.py:42
  320.1 12.3 %all-to-all-start.1 = ((f32[16,2,2,512]{3,2,1,0:T(2,128)}), f32[16,2,2,512]{3,2,1,0:T(2,128)S(1)}, u32[]{:S(2)}, u32[]{:S(2)}) async-start(f32[16,2,2,512]{3,2,1,0:T(2,128)} %get-tuple-element.185), calls=%async_computation.1 | async-start | bytes 262144 | tf_op jit(solution)/shard_map/cond/branch_1_fun/all_to_all | solution.py:42
  342.6 13.9 %all-to-all-start.2 = ((f32[16,2,4,512]{3,2,1,0:T(4,128)}), f32[16,2,4,512]{3,2,1,0:T(4,128)}, u32[]{:S(2)}, u32[]{:S(2)}) async-start(f32[16,2,4,512]{3,2,1,0:T(4,128)} %get-tuple-element.218), calls=%async_computation.2 | async-start | bytes 524288 | tf_op jit(solution)/shard_map/cond/branch_1_fun/all_to_all | solution.py:42
  363.6 12.2 %all-to-all-start.3 = ((f32[16,2,2,512]{3,2,1,0:T(2,128)}), f32[16,2,2,512]{3,2,1,0:T(2,128)}, u32[]{:S(2)}, u32[]{:S(2)}) async-start(f32[16,2,2,512]{3,2,1,0:T(2,128)} %get-tuple-element.225), calls=%async_computation.3 | async-start | bytes 262144 | tf_op jit(solution)/shard_map/cond/branch_1_fun/all_to_all | solution.py:42
  375.9 35.9 %collective-permute-start = (f32[896,512]{1,0:T(8,128)}, f32[896,512]{1,0:T(8,128)}, u32[]{:S(2)}, u32[]{:S(2)}) collective-permute-start(f32[896,512]{1,0:T(8,128)} %get-tuple-element.234), channel_id=1, source_target_pairs={{0,16},{16,0},{1,17},{17,1},{2,18},{18,2},{3,19},{19,3},{4,20},{20... | collective-permute-start | bytes 5505032 | tf_op jit(solution)/shard_map/cond/branch_1_fun/ppermute | solution.py:1015
  383.6 17.8 %all-to-all-start.4 = ((f32[16,2,2,512]{3,2,1,0:T(2,128)}), f32[16,2,2,512]{3,2,1,0:T(2,128)}, u32[]{:S(2)}, u32[]{:S(2)}) async-start(f32[16,2,2,512]{3,2,1,0:T(2,128)} %get-tuple-element.243), calls=%async_computation.4 | async-start | bytes 262144 | tf_op jit(solution)/shard_map/cond/branch_1_fun/all_to_all | solution.py:42
  401.4 8.5 %collective-permute-start.1 = (f32[768,512]{1,0:T(8,128)}, f32[768,512]{1,0:T(8,128)}, u32[]{:S(2)}, u32[]{:S(2)}) collective-permute-start(f32[768,512]{1,0:T(8,128)} %get-tuple-element.250), channel_id=1, source_target_pairs={{0,16},{16,0},{1,17},{17,1},{2,18},{18,2},{3,19},{19,3},{4,20},{20... | collective-permute-start | bytes 4718600 | tf_op jit(solution)/shard_map/cond/branch_1_fun/ppermute | solution.py:1015
  417.0 14.9 %all-to-all-start.5 = ((f32[16,2,2,512]{3,2,1,0:T(2,128)}), f32[16,2,2,512]{3,2,1,0:T(2,128)S(1)}, u32[]{:S(2)}, u32[]{:S(2)}) async-start(f32[16,2,2,512]{3,2,1,0:T(2,128)} %get-tuple-element.261), calls=%async_computation.5 | async-start | bytes 262144 | tf_op jit(solution)/shard_map/cond/branch_1_fun/all_to_all | solution.py:42
  440.6 15.3 %all-to-all-start.6 = ((f32[16,2,2,512]{3,2,1,0:T(2,128)}), f32[16,2,2,512]{3,2,1,0:T(2,128)S(1)}, u32[]{:S(2)}, u32[]{:S(2)}) async-start(f32[16,2,2,512]{3,2,1,0:T(2,128)} %get-tuple-element.275), calls=%async_computation.6 | async-start | bytes 262144 | tf_op jit(solution)/shard_map/cond/branch_1_fun/all_to_all | solution.py:42
  470.4 4.0 collective-permute-start.2
  477.5 34.0 %collective-permute-start.4 = (f32[2,400,512]{2,1,0:T(8,128)}, f32[2,400,512]{2,1,0:T(8,128)}, u32[]{:S(2)}, u32[]{:S(2)}) collective-permute-start(f32[2,400,512]{2,1,0:T(8,128)} %get-tuple-element.293), channel_id=1, source_target_pairs={{0,16},{1,17},{2,18},{3,19},{4,20},{5,21},{6,22},{7,23},{8,24},{9,... | collective-permute-start | bytes 4915208 | tf_op jit(solution)/shard_map/cond/branch_1_fun/ppermute | solution.py:1056
  480.8 34.3 %collective-permute-start.7 = (f32[768,512]{1,0:T(8,128)}, f32[768,512]{1,0:T(8,128)}, u32[]{:S(2)}, u32[]{:S(2)}) collective-permute-start(f32[768,512]{1,0:T(8,128)} %get-tuple-element.300), channel_id=1, source_target_pairs={{0,16},{1,17},{2,18},{3,19},{4,20},{5,21},{6,22},{7,23},{8,24},{9,... | collective-permute-start | bytes 4718600 | tf_op jit(solution)/shard_map/cond/branch_1_fun/ppermute | solution.py:1056
  483.2 26.6 %all-to-all-start.7 = ((f32[4,224,512]{2,1,0:T(8,128)}), f32[4,224,512]{2,1,0:T(8,128)}, u32[]{:S(2)}, u32[]{:S(2)}) async-start(f32[4,224,512]{2,1,0:T(8,128)} %bitcast.118), calls=%async_computation.7 | async-start | bytes 3670016 | tf_op jit(solution)/shard_map/cond/branch_1_fun/all_to_all | solution.py:47
  487.7 17.8 %collective-permute-start.6 = (f32[2,200,512]{2,1,0:T(8,128)}, f32[2,200,512]{2,1,0:T(8,128)}, u32[]{:S(2)}, u32[]{:S(2)}) collective-permute-start(f32[2,200,512]{2,1,0:T(8,128)} %get-tuple-element.295), channel_id=1, source_target_pairs={{0,16},{1,17},{2,18},{3,19},{4,20},{5,21},{6,22},{7,23},{8,24},{9,... | collective-permute-start | bytes 2457608 | tf_op jit(solution)/shard_map/cond/branch_1_fun/ppermute | solution.py:1056
  492.0 15.0 %collective-permute-start.5 = (f32[1,400,512]{2,1,0:T(8,128)}, f32[1,400,512]{2,1,0:T(8,128)S(1)}, u32[]{:S(2)}, u32[]{:S(2)}) collective-permute-start(f32[1,400,512]{2,1,0:T(8,128)} %slice.118), channel_id=1, source_target_pairs={{16,0},{17,1},{18,2},{19,3},{20,4},{21,5},{22,6},{23,7},{24,8},{25... | collective-permute-start | bytes 2457608 | tf_op jit(solution)/shard_map/cond/branch_1_fun/ppermute | solution.py:1057
  495.4 16.1 %collective-permute-start.3 = (f32[1,200,512]{2,1,0:T(8,128)}, f32[1,200,512]{2,1,0:T(8,128)}, u32[]{:S(2)}, u32[]{:S(2)}) collective-permute-start(f32[1,200,512]{2,1,0:T(8,128)} %slice.116), channel_id=1, source_target_pairs={{16,0},{17,1},{18,2},{19,3},{20,4},{21,5},{22,6},{23,7},{24,8},{25... | collective-permute-start | bytes 1228808 | tf_op jit(solution)/shard_map/cond/branch_1_fun/ppermute | solution.py:1057
  591.8 13.3 %collective-permute-start.19 = (f32[896,512]{1,0:T(8,128)S(1)}, f32[896,512]{1,0:T(8,128)}, u32[]{:S(2)}, u32[]{:S(2)}) collective-permute-start(f32[896,512]{1,0:T(8,128)S(1)} %get-tuple-element.512), channel_id=1, source_target_pairs={{16,0},{17,1},{18,2},{19,3},{20,4},{21,5},{22,6},{23,7},{24,8},{25... | collective-permute-start | bytes 5505032 | tf_op jit(solution)/shard_map/ppermute | solution.py:1057
  604.9 3.9 collective-permute-start.18
  (63 other events, 607.5 us)
Sparse Core Ops, SparseCore 0:
  293.0 122.7 all-reduce.5
  423.1 180.0 all-reduce.7
